TPU v7x, 512 devices: a whole 4x8x8 slice. The times are simulated.
512 devices in a mesh: ctx: 32 (over z, x_lo, core), head: 16 (over x_hi, y).
Axes of the slice: x: 4 (x_hi: 2, x_lo: 2; x = x_hi * 2 + x_lo), y: 8, z: 8, core: 2. Of those that a mesh axis runs over, the one named last changes fastest.
Arguments:
- queries: bfloat16 [6144, 4096], P('ctx', 'head'), may hold values from -30 to 30
- keys: bfloat16 [6144, 1024], P('ctx'), may hold values from -6 to 6
- values: bfloat16 [6144, 1024], P('ctx'), may hold values from -6 to 6
- out_grad: bfloat16 [6144, 4096], P('ctx', 'head'), may hold values from -6 to 6
- positions: int32 [6144], P('ctx'), may hold values from 0 to 6143, as said below
Outputs:
- query_grad: bfloat16 [6144, 4096], P('ctx', 'head')
- key_fisher: float32 [16, 64], P('head')
- value_fisher: float32 [16, 64], P('head')
Inputs may be any that keep to these rules, and one draw needn't show every extreme that they name: Each aligned block of 96 rows holds 96 consecutive positions in increasing order; the blocks' order is a permutation of all 64 blocks, so positions is a permutation of the document.
All inputs are finite; a program needn't handle non-finite values.
Results may differ from a plain program's by a relative error of at most 0.009.
The roundings to bfloat16 on the way count: a program that leaves them out, or rounds other values in their place, can miss the bound.
Values may be sent and summed in bfloat16 or wider, within the bound.
No kernel may reach another device: no remote copies, remote signals or barrier semaphores. Data moves between devices by JAX's collectives and lax.ppermute only.
A program may use at most 128 MiB of HBM per device.

v0:
```python
import math

import jax
import jax.numpy as jnp
from jax import lax
from jax.sharding import PartitionSpec as P

HD = 128
HEADS_DEV = 2
GROUP = 4


NEGATIVE_FILL = -1e30


def from_partner(value, axis, stride):
    mask = 2**stride
    pairs = [(source, source ^ mask) for source in range(lax.axis_size(axis))]
    return lax.ppermute(value, axis, pairs)


def angles_of(pos_table, width):
    half_width = width // 2
    frequency = 500000.0 ** (-(jnp.arange(half_width, dtype=jnp.float32) * 2.0 / width))
    wavelength = 2.0 * math.pi / frequency
    smooth = jnp.clip((8192.0 / wavelength - 1.0) / 3.0, 0.0, 1.0)
    frequency = (1.0 - smooth) * frequency / 8.0 + smooth * frequency
    return pos_table.astype(jnp.float32)[:, None, None] * frequency[None, None, :]


def rotate(vector, angle):
    half_width = vector.shape[-1] // 2
    leading = vector[..., :half_width]
    trailing = vector[..., half_width:]
    cosine = jnp.cos(angle)
    sin_part = jnp.sin(angle)
    return jnp.concatenate(
        [leading * cosine - trailing * sin_part, trailing * cosine + leading * sin_part], axis=-1
    )


def unrotate(vector, angle):
    half_width = vector.shape[-1] // 2
    leading = vector[..., :half_width]
    trailing = vector[..., half_width:]
    cosine = jnp.cos(angle)
    sin_part = jnp.sin(angle)
    return jnp.concatenate(
        [leading * cosine + trailing * sin_part, trailing * cosine - leading * sin_part], axis=-1
    )


def body(queries, keys, values, out_grad, positions):
    tokens = queries.shape[0]
    scale = HD ** (-0.5)
    kv_index = lax.axis_index("head") * HEADS_DEV // GROUP
    key_local = lax.dynamic_slice_in_dim(keys, kv_index * HD, HD, 1)
    value_local = lax.dynamic_slice_in_dim(values, kv_index * HD, HD, 1)
    local_angle = angles_of(positions, HD)
    query_rot = rotate(
        queries.reshape(tokens, HEADS_DEV, HD).astype(jnp.float32), local_angle
    ).astype(jnp.bfloat16)
    key_rot = rotate(key_local.astype(jnp.float32)[:, None, :], local_angle)[:, 0, :].astype(
        jnp.bfloat16
    )
    grad_heads = out_grad.reshape(tokens, HEADS_DEV, HD)
    all_positions = lax.all_gather(positions, "ctx", axis=0, tiled=True)

    def score_block(key_piece, value_piece):
        count = key_piece.shape[0]
        visible = (all_positions[None, :] <= positions[:, None])[:, None, :]
        scores = (
            jnp.einsum("thd,nd->thn", query_rot, key_piece, preferred_element_type=jnp.float32)
            * scale
        )
        dprob = jnp.einsum(
            "thd,nd->thn", grad_heads, value_piece, preferred_element_type=jnp.float32
        )
        return (visible, scores, dprob)

    pieces = (
        lax.all_gather(key_rot, "ctx", axis=0, tiled=True),
        lax.all_gather(value_local, "ctx", axis=0, tiled=True),
    )
    running = jnp.full((tokens, HEADS_DEV), NEGATIVE_FILL, jnp.float32)
    visible, scores, dprob = score_block(pieces[0], pieces[1])
    newmax = jnp.maximum(running, jnp.max(jnp.where(visible, scores, NEGATIVE_FILL), axis=-1))
    probs = jnp.where(visible, jnp.exp(scores - newmax[..., None]), 0.0)
    stats = (newmax, jnp.sum(probs, axis=-1), jnp.sum(probs * dprob, axis=-1))
    lse = stats[0] + jnp.log(stats[1])
    delta = stats[2] / stats[1]
    pieces = (
        lax.all_gather(key_rot, "ctx", axis=0, tiled=True),
        lax.all_gather(value_local, "ctx", axis=0, tiled=True),
    )
    visible, scores, dprob = score_block(pieces[0], pieces[1])
    probs = jnp.where(visible, jnp.exp(scores - lse[..., None]), 0.0)
    dscore = (probs * (dprob - delta[..., None])).astype(jnp.bfloat16)
    dq_rot = jnp.einsum("thn,nd->thd", dscore, pieces[0], preferred_element_type=jnp.float32)
    query_grad = (
        unrotate(dq_rot * scale, local_angle).reshape(tokens, HEADS_DEV * HD).astype(jnp.bfloat16)
    )
    all_stats = (
        lax.all_gather(lse, "ctx", axis=0, tiled=True),
        lax.all_gather(delta, "ctx", axis=0, tiled=True),
    )
    query_flat = query_rot.reshape(tokens, HEADS_DEV * HD)
    pieces = (
        lax.all_gather(query_flat, "ctx", axis=0, tiled=True),
        lax.all_gather(out_grad, "ctx", axis=0, tiled=True),
    )
    count = pieces[0].shape[0]
    query_heads = pieces[0].reshape(count, HEADS_DEV, HD)
    grad_piece = pieces[1].reshape(count, HEADS_DEV, HD)
    piece_lse = all_stats[0]
    piece_delta = all_stats[1]
    visible = (positions[None, :] <= all_positions[:, None])[:, None, :]
    scores = (
        jnp.einsum("nhd,td->nht", query_heads, key_rot, preferred_element_type=jnp.float32) * scale
    )
    dprob = jnp.einsum("nhd,td->nht", grad_piece, value_local, preferred_element_type=jnp.float32)
    probs = jnp.where(visible, jnp.exp(scores - piece_lse[..., None]), 0.0)
    dscore = (probs * (dprob - piece_delta[..., None])).astype(jnp.bfloat16)
    grad_value = jnp.einsum(
        "nht,nhd->td", probs.astype(jnp.bfloat16), grad_piece, preferred_element_type=jnp.float32
    )
    grad_key = jnp.einsum("nht,nhd->td", dscore, query_heads, preferred_element_type=jnp.float32)
    grad_key, grad_value = (grad_key, grad_value)
    key_pre = unrotate((grad_key * scale)[:, None, :], local_angle)[:, 0, :]
    parity = lax.axis_index("head") % 2
    half_width = HD // 2
    partner = (
        from_partner(key_pre.astype(jnp.bfloat16), "head", 0).astype(key_pre.dtype),
        from_partner(grad_value.astype(jnp.bfloat16), "head", 0).astype(grad_value.dtype),
    )
    mine_key = lax.dynamic_slice_in_dim(key_pre + partner[0], parity * half_width, half_width, 1)
    mine_value = lax.dynamic_slice_in_dim(
        grad_value + partner[1], parity * half_width, half_width, 1
    )
    totals = lax.psum(
        (jnp.sum(mine_key * mine_key, axis=0), jnp.sum(mine_value * mine_value, axis=0)), "ctx"
    )
    count_all = tokens * lax.axis_size("ctx")
    key_fisher = (totals[0] / count_all)[None, :]
    value_fisher = (totals[1] / count_all)[None, :]
    return (query_grad, key_fisher, value_fisher)


def solution(mesh):
    return jax.shard_map(
        body,
        mesh=mesh,
        in_specs=(P("ctx", "head"), P("ctx", None), P("ctx", None), P("ctx", "head"), P("ctx")),
        out_specs=(P("ctx", "head"), P("head", None), P("head", None)),
        check_vma=False,
    )
```

profile of v0, /device:TPU:1, one launch (start us, length us, event | category | flops | bytes accessed | tf_op | source)
XLA Modules:
  0.0 383.5 jit_solution(8679988982527788748)
XLA Ops:
  11.4 1.0 reshape.220
  14.5 1.3 dynamic-slice
  17.4 111.2 %all-reduce = s32[6144]{0:T(1024)S(1)} all-reduce(s32[6144]{0:T(1024)S(1)} %dynamic-update-slice), channel_id=1, replica_groups=mesh['ctx'=32,'head'=16] {'ctx'}, use_global_device_ids=true, to_apply=%add | all-reduce | flops 6144 | bytes 49152
  128.6 1.4 broadcast_compare_fusion.1
  130.0 1.8 broadcast_compare_fusion
  131.8 7.2 %select_reduce_fusion = (f32[192,2]{0,1:T(2,128)S(1)}, f32[192,2,6144]{2,0,1:T(8,128)}) fusion(pred[192,6144]{1,0:T(8,128)(4,1)S(1)} %broadcast_compare_fusion.1, bf16[6144,1,128]{2,0,1:T(8,128)(2,1)} %all-gather.14.cloned.1.call-done, bf16[192,2,64]{2,0,1:T(8,128)(2,1)S(1)} %get-tuple-element.10, bf16[192,2,64]{2,0,1:T(8,128)(2,1)S(1)} %get-tuple-element.9), kind=kOutput, calls=%fused_computation.9 | convolution fusion | flops 611253888 | bytes 12289536 | tf_op jit(solution)/shard_map/thd,nd->thn/dot_general | solution.py:73
  139.0 14.1 %all-gather.8.cloned.1.call-done = bf16[6144,128]{1,0:T(8,128)(2,1)} async-done(((bf16[192,128]{1,0:T(8,128)(2,1)}), bf16[6144,128]{1,0:T(8,128)(2,1)}) %all-gather.8.cloned.1.call-update) | async-done | bytes 1572880 | tf_op jit(solution)/shard_map/all_gather | solution.py:94
  153.0 8.4 %fusion.4 = (f32[192,2]{0,1:T(2,128)S(1)}, f32[192,2]{0,1:T(2,128)S(1)}, f32[6144,192,2]{0,1,2:T(8,128)}) fusion(f32[192,2,6144]{2,0,1:T(8,128)} %get-tuple-element.24, f32[192,2]{0,1:T(2,128)S(1)} %broadcast_maximum_fusion, pred[192,6144]{1,0:T(8,128)(4,1)S(1)} %broadcast_compare_fusion.1, bf16[6144,128]{1,0:T(8,128)(2,1)} %all-gather.8.cloned.1.call-done, ...), kind=kOutput, calls=%fused_computation.11 | convolution fusion | flops 615775488 | bytes 21729792 | tf_op jit(solution)/shard_map/thd,nd->thn/dot_general | solution.py:76
  161.4 32.6 %all-gather.1 = f32[32,192,2]{1,2,0:T(2,128)S(1)} all-gather(f32[1,192,2]{1,2,0:T(2,128)S(1)} %bitcast.106), channel_id=1, replica_groups=mesh['ctx'=32,'head'=16] {'ctx'}, dimensions={0}, use_global_device_ids=true | all-gather | bytes 50688 | tf_op jit(solution)/shard_map/all_gather | solution.py:104
  194.7 31.2 %all-gather.2 = f32[32,192,2]{1,2,0:T(2,128)S(1)} all-gather(f32[1,192,2]{1,2,0:T(2,128)S(1)} %bitcast.107), channel_id=1, replica_groups=mesh['ctx'=32,'head'=16] {'ctx'}, dimensions={0}, use_global_device_ids=true | all-gather | bytes 50688 | tf_op jit(solution)/shard_map/all_gather | solution.py:105
  226.7 8.2 %fusion.15 = f32[192,2,128]{2,0,1:T(8,128)S(1)} fusion(bf16[6144,1,128]{2,0,1:T(8,128)(2,1)S(1)} %copy-done.2, f32[6144,192,2]{0,1,2:T(8,128)} %get-tuple-element.25, f32[192,2,6144]{2,0,1:T(8,128)} %get-tuple-element.24, f32[192,2]{0,1:T(2,128)S(1)} %get-tuple-element.20, f32[192,2]{0,1:T(2,128)S(1)} %get-tuple-element.19, ...), kind=kOutput, calls=%fused_computation.23 | convolution fusion | flops 615825408 | bytes 21826560 | tf_op jit(solution)/shard_map/thn,nd->thd/dot_general | solution.py:99
  235.6 3.2 copy.25
  238.8 6.7 %exponential_select_fusion = f32[6144,2,192]{0,2,1:T(8,128)} fusion(bf16[6144,2,128]{0,2,1:T(8,128)(2,1)S(1)} %bitcast.102, f32[6144,2]{0,1:T(2,128)} %reshape.227, pred[6144,192]{0,1:T(8,128)(4,1)} %broadcast_compare_fusion, bf16[192,64]{1,0:T(8,128)(2,1)} %bitcast.105, bf16[192,64]{1,0:T(8,128)(2,1)} %bitcast.104), kind=kOutput, calls=%fused_computation.7 | convolution fusion | flops 611155968 | bytes 13860864 | tf_op jit(solution)/shard_map/nhd,td->nht/dot_general | solution.py:119
  245.5 49.3 %all-gather.12.cloned.1.call-done = bf16[6144,256]{1,0:T(8,128)(2,1)} async-done(((bf16[192,256]{1,0:T(8,128)(2,1)}), bf16[6144,256]{1,0:T(8,128)(2,1)}) %all-gather.12.cloned.1.call-update) | async-done | bytes 3145744 | tf_op jit(solution)/shard_map/all_gather | solution.py:110
  294.8 3.2 copy.28
  298.0 5.7 %fusion.54 = (bf16[192,128]{1,0:T(8,128)(2,1)}, f32[192,128]{1,0:T(8,128)}) fusion(bf16[6144,2,128]{0,2,1:T(8,128)(2,1)S(1)} %bitcast.100, f32[6144,2,192]{0,2,1:T(8,128)} %exponential_select_fusion), kind=kOutput, calls=%fused_computation.79 | convolution fusion | flops 606363648 | bytes 12730368 | tf_op jit(solution)/shard_map/nht,nhd->td/dot_general | solution.py:124
  303.8 8.0 %fusion.22 = f32[192,1,128]{2,0,1:T(8,128)} fusion(bf16[6144,2,128]{0,2,1:T(8,128)(2,1)} %bitcast.103, f32[6144,2,192]{0,2,1:T(8,128)} %exponential_select_fusion, bf16[6144,2,128]{0,2,1:T(8,128)(2,1)S(1)} %bitcast.101, f32[6144,2]{0,1:T(2,128)} %reshape.229, bf16[192,128]{1,0:T(8,128)(2,1)} %constant_dynamic-slice_fusion), kind=kOutput, calls=%fused_computation.26 | convolution fusion | flops 1215062016 | bytes 15925248 | tf_op jit(solution)/shard_map/nht,nhd->td/dot_general | solution.py:127
  311.7 1.4 fusion.38
  313.2 3.1 collective-permute-start
  316.4 2.2 collective-permute-start.1
  318.5 1.7 copy_bitcast_fusion.1
  320.3 1.1 collective-permute-done.1
  321.4 1.0 fusion.43
  322.4 54.0 %all-reduce.1 = (f32[64]{0:T(128)S(1)}, f32[64]{0:T(128)S(1)}) all-reduce(f32[64]{0:T(128)S(1)} %fusion.45, f32[64]{0:T(128)S(1)} %fusion.43), channel_id=1, replica_groups=mesh['ctx'=32,'head'=16] {'ctx'}, use_global_device_ids=true, to_apply=%region_4.5 | all-reduce | flops 128 | bytes 1024 | tf_op jit(solution)/shard_map/psum | solution.py:140
  (47 shorter events, 10.1 us)
Async XLA Ops:
  7.2 3.5 copy-start
  7.2 122.8 %copy-start.6 = (s32[192]{0:T(256)S(1)}, s32[192]{0:T(256)}, u32[]{:S(2)}) copy-start(s32[192]{0:T(256)} %param.9) | copy-start | bytes 2308
  7.2 124.6 %all-gather.14.cloned.1.call-start = ((), (), s32[]{:S(2)}) async-start(), calls=%async_computation.3 | async-start | bytes 1622016 | tf_op jit(solution)/shard_map/all_gather | solution.py:93
  9.2 0.6 copy-start.4
  9.3 0.6 copy-start.5
  10.6 142.4 %all-gather.8.cloned.1.call-start = ((), (), s32[]{:S(2)}) async-start(), calls=%async_computation | async-start | bytes 1622016 | tf_op jit(solution)/shard_map/all_gather | solution.py:94
  11.4 224.3 %all-gather.10.cloned.1.call-start = ((), (), s32[]{:S(2)}) async-start(), calls=%async_computation.1 | async-start | bytes 3244032 | tf_op jit(solution)/shard_map/all_gather | solution.py:109
  13.9 280.9 %all-gather.12.cloned.1.call-start = ((), (), s32[]{:S(2)}) async-start(), calls=%async_computation.2 | async-start | bytes 3244032 | tf_op jit(solution)/shard_map/all_gather | solution.py:110
  131.8 21.3 %copy-start.3 = (bf16[192,256]{1,0:T(8,128)(2,1)S(1)}, bf16[192,256]{1,0:T(8,128)(2,1)}, u32[]{:S(2)}) copy-start(bf16[192,256]{1,0:T(8,128)(2,1)} %param.8) | copy-start | bytes 294916
  153.0 73.6 %copy-start.2 = (bf16[6144,1,128]{2,0,1:T(8,128)(2,1)S(1)}, bf16[6144,1,128]{2,0,1:T(8,128)(2,1)}, u32[]{:S(2)}) copy-start(bf16[6144,1,128]{2,0,1:T(8,128)(2,1)} %all-gather.14.cloned.1.call-done) | copy-start | bytes 4718596
  238.8 6.7 %copy-start.1 = (bf16[6144,256]{0,1:T(8,128)(2,1)}, bf16[6144,256]{0,1:T(8,128)(2,1)S(1)}, u32[]{:S(2)}) copy-start(bf16[6144,256]{0,1:T(8,128)(2,1)S(1)} %copy.25) | copy-start | bytes 9437188
  313.2 7.0 %collective-permute-start = (bf16[192,128]{1,0:T(8,128)(2,1)S(1)}, bf16[192,128]{1,0:T(8,128)(2,1)S(1)}, u32[]{:S(2)}, u32[]{:S(2)}) collective-permute-start(bf16[192,128]{1,0:T(8,128)(2,1)S(1)} %get-tuple-element.7), channel_id=1, source_target_pairs={{0,1},{1,0},{2,3},{3,2},{4,5},{5,4},{6,7},{7,6},{8,9},{9,8},{10,11... | collective-permute-start | bytes 147464 | tf_op jit(solution)/shard_map/ppermute | solution.py:19
  316.4 5.0 %collective-permute-start.1 = (bf16[192,128]{1,0:T(8,128)(2,1)}, bf16[192,128]{1,0:T(8,128)(2,1)S(1)}, u32[]{:S(2)}, u32[]{:S(2)}) collective-permute-start(bf16[192,128]{1,0:T(8,128)(2,1)} %get-tuple-element.26), channel_id=1, source_target_pairs={{0,1},{1,0},{2,3},{3,2},{4,5},{5,4},{6,7},{7,6},{8,9},{9,8},{10,11... | collective-permute-start | bytes 147464 | tf_op jit(solution)/shard_map/ppermute | solution.py:19
Sparse Core Ops, SparseCore 0:
  10.7 73.2 all-gather.13
  86.2 66.7 all-gather.7
  155.8 68.3 all-gather.9
  226.2 68.5 all-gather.11
where the time goes:
time: 384 us
  blocking collectives  229 us (60%)
  waiting for transfers between devices  65 us (17%)
  matrix products  44.1 us (11%)
  between operations  14.6 us (4%)
  other arithmetic  12.7 us (3%)
  local copies, waits for them, and re-layouts  12.5 us (3%)
  starting transfers between devices  5.44 us (1%)
    unnamed x1, blocking collectives  111 us
    psum x1, blocking collectives, body(): lax.psum((jnp.sum(mine_key * mine_key, axis=0), jnp.sum(mine_value * mine...  54 us
    all_gather x1, waiting for transfers between devices, body(): lax.all_gather(out_grad, 'ctx', axis=0, tiled=True)  49.3 us
    all_gather x1, blocking collectives, body(): lax.all_gather(lse, 'ctx', axis=0, tiled=True)  32.6 us
    all_gather x1, blocking collectives, body(): lax.all_gather(delta, 'ctx', axis=0, tiled=True)  31.2 us
    all_gather x1, waiting for transfers between devices, body(): lax.all_gather(value_local, 'ctx', axis=0, tiled=True)  14.1 us
    dot_general x1, matrix products, score_block(): jnp.einsum('thd,nd->thn', grad_heads, value_piece, preferred_element_type...  8.39 us
    dot_general x1, matrix products, body(): jnp.einsum('thn,nd->thd', dscore, pieces[0], preferred_element_type=jnp.f...  8.16 us
  transfers between devices with their start and end apart: 6, of which 3 were waited for; matrix products, arithmetic and copies ran while one was open for 12% of the time, Pallas kernels for 0%

commit v1 on v0

v1 whole, which is shorter than its diff:
```python
import functools
import math

import jax
import jax.numpy as jnp
import numpy as np
from jax import lax
from jax.experimental import pallas as pl
from jax.experimental.pallas import tpu as pltpu
from jax.sharding import Mesh
from jax.sharding import PartitionSpec as P

HD = 128
SEQ = 6144
BLOCK = 96
TOK = 192
PACK = TOK + 16
SCALE = HD ** (-0.5)
LOG2E = math.log2(math.e)
FILL = -1e30
FLOOR = -1e29
MIB = 1024 * 1024
VMEM = 20 * MIB
VMEM_LARGE = 40 * MIB
VMEM_ALL = 60 * MIB
ROWS = 2 * TOK + 16
AX_Z, AX_X, AX_C = "z", "xl", "core"
QGROUP = (AX_X, AX_C)
KGROUP = (AX_Z, "yl")
ALLGROUP = (AX_Z, AX_X, AX_C, "yl")
NQ = 4
NK = 8
NALL = 2 * NQ * NK
QL = 2 * NQ * TOK
STAT = QL // HD
QT = 384


def frequencies():
    half = HD // 2
    freq = np.float32(500000.0) ** (-(np.arange(half, dtype=np.float32) * np.float32(2.0) / np.float32(HD)))
    freq = freq.astype(np.float32)
    wave = (np.float32(2.0 * math.pi) / freq).astype(np.float32)
    smooth = np.clip((np.float32(8192.0) / wave - np.float32(1.0)) / np.float32(3.0), 0.0, 1.0).astype(np.float32)
    freq = (np.float32(1.0) - smooth) * freq / np.float32(8.0) + smooth * freq
    return np.concatenate([freq, freq]).astype(np.float32)[None, :]


def dot(a, b, ca, cb):
    return lax.dot_general(a, b, (((ca,), (cb,)), ((), ())), preferred_element_type=jnp.float32)


def smem():
    return pl.BlockSpec(memory_space=pltpu.SMEM)


def vmem():
    return pl.BlockSpec(memory_space=pltpu.VMEM)


def rotate(x, cosine, sine):
    x = x.astype(jnp.float32)
    return (x * cosine + pltpu.roll(x, HD // 2, 1) * sine).astype(jnp.bfloat16)


def id_rows(pos_ref, j):
    block = lax.div(pos_ref[j * BLOCK], BLOCK).astype(jnp.float32)
    return jnp.full((PACK - TOK, HD), block, jnp.float32).astype(jnp.bfloat16)


def key_kernel(kvi_ref, pos_ref, freq_ref, k_ref, v_ref, kv_ref, cs_ref):
    row = lax.broadcasted_iota(jnp.int32, (TOK, HD), 0)
    pos = jnp.where(row < BLOCK, pos_ref[0] + row, pos_ref[BLOCK] + row - BLOCK)
    angle = pos.astype(jnp.float32) * freq_ref[...]
    cosine = jnp.cos(angle)
    lane = lax.broadcasted_iota(jnp.int32, (TOK, HD), 1)
    sine = jnp.sin(angle)
    sine = jnp.where(lane < HD // 2, -sine, sine)
    cs_ref[0] = cosine
    cs_ref[1] = sine
    key = rotate(k_ref[...], cosine, sine)
    lanes = lax.broadcasted_iota(jnp.int32, (ROWS - 2 * TOK, HD), 1)
    first, second = (lax.div(pos_ref[j * BLOCK], BLOCK) for j in range(2))
    ids = jnp.where(lanes < HD // 2, first, second).astype(jnp.float32).astype(jnp.bfloat16)
    for i in range(NK):
        kv_ref[i, :TOK, :] = key
        kv_ref[i, TOK : 2 * TOK, :] = v_ref[...]
        kv_ref[i, 2 * TOK :, :] = ids


def prep_keys(kvi, positions, freq, keys, values):
    whole = lambda *shape: pl.BlockSpec(shape, lambda i, kvi, pos: (0,) * len(shape))
    picked = pl.BlockSpec((TOK, HD), lambda i, kvi, pos: (0, kvi[0]))
    return pl.pallas_call(
        key_kernel,
        grid_spec=pltpu.PrefetchScalarGridSpec(
            num_scalar_prefetch=2,
            grid=(1,),
            in_specs=[whole(1, HD), picked, picked],
            out_specs=[whole(NK, ROWS, HD), whole(2, TOK, HD)],
        ),
        out_shape=[
            jax.ShapeDtypeStruct((NK, ROWS, HD), jnp.bfloat16),
            jax.ShapeDtypeStruct((2, TOK, HD), jnp.float32),
        ],
        compiler_params=pltpu.CompilerParams(vmem_limit_bytes=VMEM_ALL),
        cost_estimate=pl.CostEstimate(flops=10**6, bytes_accessed=10**6, transcendentals=10**5),
        name="rotate_keys",
    )(kvi, positions, freq, keys, values)


def query_kernel(pos_ref, cs_ref, q_ref, g_ref, qg_ref):
    for head in range(2):
        cols = slice(head * HD, (head + 1) * HD)
        qg_ref[:TOK, cols] = rotate(q_ref[:, cols], cs_ref[0], cs_ref[1])
    qg_ref[:TOK, 2 * HD :] = g_ref[...]
    for j in range(4):
        qg_ref[TOK:, j * HD : (j + 1) * HD] = id_rows(pos_ref, j % 2)


def prep_queries(positions, cs, queries, out_grad):
    return pl.pallas_call(
        query_kernel,
        in_specs=[smem()] + [vmem()] * 3,
        out_specs=vmem(),
        out_shape=jax.ShapeDtypeStruct((PACK, 4 * HD), jnp.bfloat16),
        compiler_params=pltpu.CompilerParams(vmem_limit_bytes=VMEM),
        cost_estimate=pl.CostEstimate(flops=10**6, bytes_accessed=10**6, transcendentals=0),
        name="rotate_queries",
    )(positions, cs, queries, out_grad)


def block_id(ref, column):
    rows = ref[TOK:PACK, column * HD : (column + 1) * HD]
    return jnp.max(rows.astype(jnp.float32)).astype(jnp.int32)


def key_ids(kv_ref, c):
    rows = kv_ref[c, 2 * TOK :, :].astype(jnp.float32)
    lanes = lax.broadcasted_iota(jnp.int32, rows.shape, 1)
    masked = (jnp.where(lanes < HD // 2, rows, 0.0), jnp.where(lanes < HD // 2, 0.0, rows))
    return [jnp.max(x).astype(jnp.int32) for x in masked]


def ranks_of(ids):
    count = len(ids)
    return [sum((ids[i] < ids[j]).astype(jnp.int32) for i in range(count) if i != j) for j in range(count)]


def query_positions(perm_ref, first):
    lane = lax.broadcasted_iota(jnp.int32, (1, QL - first * QT), 1)
    pos = jnp.zeros(lane.shape, jnp.int32)
    for r in range(2 * first, 2 * NQ):
        for head in range(2):
            start = (r - 2 * first) * TOK + head * BLOCK
            pos = jnp.where(lane >= start, perm_ref[8 + r] * BLOCK - start + lane, pos)
    return pos


def key_positions(perm_ref, pair):
    row = lax.broadcasted_iota(jnp.int32, (TOK, 1), 0)
    low, high = perm_ref[32 + 2 * pair], perm_ref[33 + 2 * pair]
    return row + jnp.where(row < BLOCK, low * BLOCK, (high - 1) * BLOCK)


def first_tile(perm_ref, pair):
    low = perm_ref[32 + 2 * pair]
    return sum((perm_ref[9 + 2 * t] < low).astype(jnp.int32) for t in range(NQ))


def block_rows(start, count):
    return pl.ds(pl.multiple_of(start, BLOCK), count)


def stats_kernel(q0, q1, q2, q3, kv_ref, st_ref, qs_ref, gs_ref, ks_ref, vs_ref, perm_ref, m_ref, l_ref, a_ref):
    slots = (q0, q1, q2, q3)
    ids = [block_id(ref, j) for ref in slots for j in range(2)]
    for j, r in enumerate(ranks_of(ids)):
        perm_ref[r] = j
        perm_ref[8 + r] = ids[j]
        ref, rows = slots[j // 2], slice((j % 2) * BLOCK, (j % 2 + 1) * BLOCK)
        for head in range(2):
            to = block_rows(r * TOK + head * BLOCK, BLOCK)
            qs_ref[to, :] = ref[rows, head * HD : (head + 1) * HD]
            gs_ref[to, :] = ref[rows, (2 + head) * HD : (3 + head) * HD]
    ids = [x for c in range(NK) for x in key_ids(kv_ref, c)]
    for j, r in enumerate(ranks_of(ids)):
        perm_ref[16 + r] = j
        perm_ref[32 + r] = ids[j]
        rows = slice((j % 2) * BLOCK, (j % 2 + 1) * BLOCK)
        to = block_rows(r * BLOCK, BLOCK)
        ks_ref[to, :] = kv_ref[j // 2, rows, :]
        vs_ref[to, :] = kv_ref[j // 2, slice(TOK + rows.start, TOK + rows.stop), :]
    m_ref[...] = jnp.full(m_ref.shape, FLOOR, jnp.float32)
    l_ref[...] = jnp.zeros(l_ref.shape, jnp.float32)
    a_ref[...] = jnp.zeros(a_ref.shape, jnp.float32)

    def step(pair, _):
        rows = block_rows(pair * TOK, TOK)
        tile = first_tile(perm_ref, pair)
        for first in range(NQ):

            @pl.when(tile == first)
            def _():
                cols = slice(first * QT, QL)
                s = dot(ks_ref[rows, :], qs_ref[cols, :], 1, 1) * (SCALE * LOG2E)
                d = dot(vs_ref[rows, :], gs_ref[cols, :], 1, 1)
                visible = key_positions(perm_ref, pair) <= query_positions(perm_ref, first)
                s = jnp.where(visible, s, FILL)
                m = m_ref[:, cols]
                m2 = jnp.maximum(m, jnp.max(s, axis=0, keepdims=True))
                p = jnp.exp2(s - m2)
                alpha = jnp.exp2(m - m2)
                m_ref[:, cols] = m2
                l_ref[:, cols] = alpha * l_ref[:, cols] + jnp.sum(p, axis=0, keepdims=True)
                a_ref[:, cols] = alpha * a_ref[:, cols] + jnp.sum(p * d, axis=0, keepdims=True)

        return 0

    lax.fori_loop(0, NK, step, 0)
    l = l_ref[...]
    seen = l > 0.0
    safe = jnp.where(seen, l, 1.0)
    m_ref[...] = jnp.where(seen, m_ref[...] + jnp.log2(safe), FLOOR)
    a_ref[...] = jnp.where(seen, a_ref[...] / safe, 0.0)
    for c in range(STAT):
        cols = slice(c * HD, (c + 1) * HD)
        lse, delta = m_ref[:, cols], a_ref[:, cols]
        for i in range(NQ):
            st_ref[i, c : c + 1, :] = lse
            st_ref[i, STAT + c : STAT + c + 1, :] = delta


def stats(slots, kv):
    rows = jax.ShapeDtypeStruct((QL, HD), jnp.bfloat16)
    return pl.pallas_call(
        stats_kernel,
        in_specs=[vmem()] * 5,
        out_specs=[vmem()] * 5 + [smem()],
        out_shape=[
            jax.ShapeDtypeStruct((NQ, 2 * STAT, HD), jnp.float32),
            rows,
            rows,
            rows,
            rows,
            jax.ShapeDtypeStruct((64,), jnp.int32),
        ],
        scratch_shapes=[pltpu.VMEM((1, QL), jnp.float32)] * 3,
        compiler_params=pltpu.CompilerParams(vmem_limit_bytes=VMEM_LARGE),
        cost_estimate=pl.CostEstimate(flops=12 * 10**8, bytes_accessed=2 * 10**6, transcendentals=24 * 10**5),
        name="softmax_stats",
    )(*slots, kv)


def grad_kernel(perm_ref, qs_ref, gs_ref, ks_ref, vs_ref, st_ref, dkv_ref, keep_ref, send_ref, dqt_ref, lse_ref, delta_ref):
    ms = [st_ref[i, :STAT, :] for i in range(NQ)]
    m = functools.reduce(jnp.maximum, ms)
    w = [jnp.exp2(x - m) for x in ms]
    l = sum(w)
    lse = m + jnp.log2(l)
    delta = sum(w[i] * st_ref[i, STAT:, :] for i in range(NQ)) / l
    for c in range(STAT):
        lse_ref[:, c * HD : (c + 1) * HD] = lse[c : c + 1, :]
        delta_ref[:, c * HD : (c + 1) * HD] = delta[c : c + 1, :]
    dqt_ref[...] = jnp.zeros(dqt_ref.shape, jnp.float32)

    def step(pair, _):
        rows = block_rows(pair * TOK, TOK)
        tile = first_tile(perm_ref, pair)
        low, high = perm_ref[16 + 2 * pair], perm_ref[17 + 2 * pair]
        for first in range(NQ):

            @pl.when(tile == first)
            def _():
                cols = slice(first * QT, QL)
                k, q, g = ks_ref[rows, :], qs_ref[cols, :], gs_ref[cols, :]
                s = dot(k, q, 1, 1) * (SCALE * LOG2E)
                d = dot(vs_ref[rows, :], g, 1, 1)
                visible = key_positions(perm_ref, pair) <= query_positions(perm_ref, first)
                s = jnp.where(visible, s, FILL)
                p = jnp.exp2(s - lse_ref[:, cols])
                ds = (p * (d - delta_ref[:, cols])).astype(jnp.bfloat16)
                dv = dot(p.astype(jnp.bfloat16), g, 1, 0).astype(jnp.bfloat16)
                dk = dot(ds, q, 1, 0).astype(jnp.bfloat16)
                dqt_ref[:, cols] += dot(k, ds, 0, 0)
                dkv_ref[low, :, :HD] = dk[:BLOCK]
                dkv_ref[low, :, HD:] = dv[:BLOCK]
                dkv_ref[high, :, :HD] = dk[BLOCK:]
                dkv_ref[high, :, HD:] = dv[BLOCK:]

        @pl.when(tile == NQ)
        def _():
            empty = jnp.zeros((BLOCK, 2 * HD), jnp.bfloat16)
            dkv_ref[low] = empty
            dkv_ref[high] = empty

        return 0

    lax.fori_loop(0, NK, step, 0)
    for t in range(NQ):
        part = dqt_ref[:, t * QT : (t + 1) * QT].T
        for i in range(2):
            block = perm_ref[2 * t + i]
            both = jnp.concatenate(
                [part[(2 * i + head) * BLOCK : (2 * i + head + 1) * BLOCK] for head in range(2)], axis=1
            )

            @pl.when(block < NQ)
            def _():
                keep_ref[block] = both

            @pl.when(block >= NQ)
            def _():
                send_ref[block - NQ] = both


def grads(perm, qs, gs, ks, vs, st):
    half = jax.ShapeDtypeStruct((NQ, BLOCK, 2 * HD), jnp.float32)
    return pl.pallas_call(
        grad_kernel,
        in_specs=[smem()] + [vmem()] * 5,
        out_specs=[vmem()] * 3,
        out_shape=[jax.ShapeDtypeStruct((2 * NK, BLOCK, 2 * HD), jnp.bfloat16), half, half],
        scratch_shapes=[
            pltpu.VMEM((HD, QL), jnp.float32),
            pltpu.VMEM((1, QL), jnp.float32),
            pltpu.VMEM((1, QL), jnp.float32),
        ],
        compiler_params=pltpu.CompilerParams(vmem_limit_bytes=VMEM_LARGE),
        cost_estimate=pl.CostEstimate(flops=30 * 10**8, bytes_accessed=3 * 10**6, transcendentals=24 * 10**5),
        name="tile_gradients",
    )(perm, qs, gs, ks, vs, st)


def dq_kernel(a_ref, b_ref, c_ref, cs_ref, out_ref):
    for j in range(2):
        rows = slice(j * BLOCK, (j + 1) * BLOCK)
        cosine, sine = cs_ref[0, rows, :], cs_ref[1, rows, :]
        for head in range(2):
            cols = slice(head * HD, (head + 1) * HD)
            x = (a_ref[j, :, cols] + b_ref[j, :, cols] + c_ref[j, :, cols]) * SCALE
            out_ref[rows, cols] = (x * cosine - pltpu.roll(x, HD // 2, 1) * sine).astype(jnp.bfloat16)


def finish_dq(kept, near, far, cs):
    return pl.pallas_call(
        dq_kernel,
        in_specs=[vmem()] * 4,
        out_specs=vmem(),
        out_shape=jax.ShapeDtypeStruct((TOK, 2 * HD), jnp.bfloat16),
        compiler_params=pltpu.CompilerParams(vmem_limit_bytes=VMEM),
        cost_estimate=pl.CostEstimate(flops=10**6, bytes_accessed=10**6, transcendentals=0),
        name="query_gradient",
    )(kept, near, far, cs)


def square_kernel(yl_ref, parts_ref, cs_ref, out_ref):
    rows = pl.ds(pl.multiple_of(yl_ref[0] * BLOCK, BLOCK), BLOCK)
    cosine, sine = cs_ref[0, rows, :], cs_ref[1, rows, :]
    total = sum(parts_ref[i].astype(jnp.float32) for i in range(2 * NK))
    x = total[:, :HD] * SCALE
    y = total[:, HD:]
    x = x * cosine - pltpu.roll(x, HD // 2, 1) * sine
    x = jnp.sum(x * x, axis=0, keepdims=True)
    y = jnp.sum(y * y, axis=0, keepdims=True)
    out_ref[:, 0:1, :] = jnp.broadcast_to(x[None], (NALL, 1, HD))
    out_ref[:, 1:2, :] = jnp.broadcast_to(y[None], (NALL, 1, HD))


def squares(yl, parts, cs):
    return pl.pallas_call(
        square_kernel,
        in_specs=[smem(), vmem(), vmem()],
        out_specs=vmem(),
        out_shape=jax.ShapeDtypeStruct((NALL, 2, HD), jnp.float32),
        compiler_params=pltpu.CompilerParams(vmem_limit_bytes=VMEM),
        cost_estimate=pl.CostEstimate(flops=10**6, bytes_accessed=10**6, transcendentals=0),
        name="square_sums",
    )(yl, parts, cs)


def swap(value, axis):
    return lax.ppermute(value, axis, [(0, 1), (1, 0)])


def body(queries, keys, values, out_grad, positions):
    kvi = (lax.axis_index("xh") * 4 + lax.axis_index("yh")).astype(jnp.int32).reshape(1)
    yl = lax.axis_index("yl").astype(jnp.int32)
    freq = jnp.asarray(frequencies())
    kv, cs = prep_keys(kvi, positions, freq, keys, values)
    kv_all = lax.all_to_all(kv, AX_Z, 0, 0)
    qg = prep_queries(positions, cs, queries, out_grad)
    other_x = swap(qg, AX_X)
    other_core = swap(qg, AX_C)
    other_both = swap(other_x, AX_C)
    st, qs, gs, ks, vs, perm = stats((qg, other_x, other_core, other_both), kv_all)
    st_all = lax.all_to_all(st, QGROUP, 0, 0)
    dkv, keep, send = grads(perm, qs, gs, ks, vs, st_all)
    near = swap(send, AX_C)
    far = swap(keep[2:] + near[2:], AX_X)
    parts = lax.all_to_all(dkv, KGROUP, 0, 0)
    sums = lax.all_to_all(squares(yl.reshape(1), parts, cs), ALLGROUP, 0, 0)
    sums = jnp.sum(sums, axis=0)
    query_grad = finish_dq(keep[:2], near[:2], far, cs)
    mine = lax.dynamic_slice_in_dim(sums, yl * (HD // 2), HD // 2, 1) / SEQ
    return query_grad, mine[0:1], mine[1:2]


def solution(mesh):
    inner = Mesh(
        mesh.devices.reshape(8, 2, 2, 2, 4, 2), (AX_Z, AX_X, AX_C, "xh", "yh", "yl")
    )
    ctx, head = (AX_Z, AX_X, AX_C), ("xh", "yh", "yl")
    return jax.shard_map(
        body,
        mesh=inner,
        in_specs=(P(ctx, head), P(ctx, None), P(ctx, None), P(ctx, head), P(ctx)),
        out_specs=(P(ctx, head), P(head, None), P(head, None)),
        check_vma=False,
    )
```

time: 384 us -> 101 us (0.26)
  blocking collectives: 229 us -> 5.81 us
  matrix products: 44.1 us -> 0 us
  starting transfers between devices: 5.44 us -> 36.9 us
  waiting for transfers between devices: 65 us -> 37.3 us
  Pallas kernels: 0 us -> 17.9 us
  between operations: 14.6 us -> 0.77 us
  other arithmetic: 12.7 us -> 0.21 us
  local copies, waits for them, and re-layouts: 12.5 us -> 1.18 us
    unnamed x1 -> x0, blocking collectives: 111 us -> none
    all_gather x2 -> x0, blocking collectives: 63.8 us -> none  [the longest x1 32.6 us: body(): lax.all_gather(lse, 'ctx', axis=0, tiled=True)]
    all_gather x4 -> x0, waiting for transfers between devices: 63.4 us -> none  [the longest x1 49.3 us: body(): lax.all_gather(out_grad, 'ctx', axis=0, tiled=True)]
    psum x1 -> x0, blocking collectives: 54 us -> none  [body(): lax.psum((jnp.sum(mine_key * mine_key, axis=0), jnp.sum(mine_value * mine...]
    dot_general x6 -> x0, matrix products: 44.1 us -> none  [the longest x1 8.39 us: score_block(): jnp.einsum('thd,nd->thn', grad_heads, value_piece, preferred_element_type...]
    all_to_all x0 -> x3, waiting for transfers between devices: none -> 33.4 us  [the longest x1 14.8 us: body(): parts = lax.all_to_all(dkv, KGROUP, 0, 0)]
    all_to_all x0 -> x3, starting transfers between devices: none -> 22.2 us  [the longest x1 11 us: body(): kv_all = lax.all_to_all(kv, AX_Z, 0, 0)]
    pallas_call x0 -> x6, Pallas kernels: none -> 17.9 us  [the longest x1 7.73 us: grads(): pl.pallas_call(grad_kernel, in_specs=[smem()] + [vmem()] * 5, out_specs=[...]
  transfers between devices with their start and end apart: 6 -> 8, of which waited for: 3 -> 6; matrix products, arithmetic and copies ran while one was open for 12% -> 0% of each run, Pallas kernels for 0% -> 2%
where the time goes in v1:
time: 101 us; the launch traced here: 100 us
  waiting for transfers between devices  37.3 us (37%)
  starting transfers between devices  36.9 us (37%)
  Pallas kernels  17.9 us (18%)
  blocking collectives  5.81 us (6%)
  local copies, waits for them, and re-layouts  1.18 us (1%)
    all_to_all x1, waiting for transfers between devices, body(): parts = lax.all_to_all(dkv, KGROUP, 0, 0)  14.8 us
    ppermute x5, starting transfers between devices, swap(): return lax.ppermute(value, axis, [(0, 1), (1, 0)])  14.7 us
    all_to_all x1, starting transfers between devices, body(): kv_all = lax.all_to_all(kv, AX_Z, 0, 0)  11 us
    all_to_all x1, waiting for transfers between devices, body(): kv_all = lax.all_to_all(kv, AX_Z, 0, 0)  10.4 us
    all_to_all x1, waiting for transfers between devices, body(): sums = lax.all_to_all(squares(yl.reshape(1), parts, cs), ALLGROUP, 0, 0)  8.28 us
    pallas_call x1, Pallas kernels, grads(): pl.pallas_call(grad_kernel, in_specs=[smem()] + [vmem()] * 5, out_specs=[...  7.73 us
    all_to_all x1, starting transfers between devices, body(): sums = lax.all_to_all(squares(yl.reshape(1), parts, cs), ALLGROUP, 0, 0)  6.45 us
    all_to_all x1, blocking collectives, body(): st_all = lax.all_to_all(st, QGROUP, 0, 0)  5.81 us
  transfers between devices with their start and end apart: 8, of which 6 were waited for; matrix products, arithmetic and copies ran while one was open for 0% of the time, Pallas kernels for 2%

profile of v1, /device:TPU:1, one launch (start us, length us, event | category | flops | bytes accessed | tf_op | source)
XLA Modules:
  0.0 100.1 jit_solution(76643796626703873)
XLA Ops:
  0.6 2.9 %rotate_keys.1 = (bf16[8,400,128]{2,1,0:T(8,128)(2,1)}, f32[2,192,128]{2,1,0:T(8,128)}) custom-call(s32[1]{0:T(128)} %bitcast.kvi_ref, s32[192]{0:T(256)} %pos_ref.3, f32[1,128]{1,0:T(1,128)} %constant.26.clone.freq_ref, bf16[192,1024]{1,0:T(8,128)(2,1)} %k_ref.1, bf16[192,1024]{1,0:T(8,128)(2,1)} %v_ref.1), custom_call_target="tpu_custom_call" | custom-call | flops 1000000 | bytes 1000000 | tf_op jit(solution)/shard_map/rotate_keys/pallas_call | solution.py:94
  3.6 11.0 %all-to-all-start = ((bf16[8,400,128]{2,1,0:T(8,128)(2,1)}), bf16[8,400,128]{2,1,0:T(8,128)(2,1)S(1)}, u32[]{:S(2)}, u32[]{:S(2)}) async-start(bf16[8,400,128]{2,1,0:T(8,128)(2,1)} %get-tuple-element.15), calls=%async_computation | async-start | bytes 1638400 | tf_op jit(solution)/shard_map/all_to_all | solution.py:391
  14.6 0.6 copy-done.3
  15.3 0.6 rotate_queries.1.q0
  15.9 3.1 %collective-permute-start = (bf16[208,512]{1,0:T(8,128)(2,1)S(1)}, bf16[208,512]{1,0:T(8,128)(2,1)S(1)}, u32[]{:S(2)}, u32[]{:S(2)}) collective-permute-start(bf16[208,512]{1,0:T(8,128)(2,1)S(1)} %rotate_queries.1.q0), channel_id=1, source_target_pairs={{0,32},{32,0},{1,33},{33,1},{2,34},{34,2},{3,35},{35,3},{4,36},{36... | collective-permute-start | bytes 638984 | tf_op jit(solution)/shard_map/ppermute | solution.py:383
  19.0 3.1 %collective-permute-start.1 = (bf16[208,512]{1,0:T(8,128)(2,1)S(1)}, bf16[208,512]{1,0:T(8,128)(2,1)S(1)}, u32[]{:S(2)}, u32[]{:S(2)}) collective-permute-start(bf16[208,512]{1,0:T(8,128)(2,1)S(1)} %rotate_queries.1.q0), channel_id=1, source_target_pairs={{0,16},{16,0},{1,17},{17,1},{2,18},{18,2},{3,19},{19,3},{4,20},{20... | collective-permute-start | bytes 638984 | tf_op jit(solution)/shard_map/ppermute | solution.py:383
  22.2 1.4 %collective-permute-done.q1 = bf16[208,512]{1,0:T(8,128)(2,1)S(1)} collective-permute-done((bf16[208,512]{1,0:T(8,128)(2,1)S(1)}, bf16[208,512]{1,0:T(8,128)(2,1)S(1)}, u32[]{:S(2)}, u32[]{:S(2)}) %collective-permute-start) | collective-permute-done | bytes 213024 | tf_op jit(solution)/shard_map/ppermute | solution.py:383
  23.6 3.8 %collective-permute-start.2 = (bf16[208,512]{1,0:T(8,128)(2,1)S(1)}, bf16[208,512]{1,0:T(8,128)(2,1)S(1)}, u32[]{:S(2)}, u32[]{:S(2)}) collective-permute-start(bf16[208,512]{1,0:T(8,128)(2,1)S(1)} %collective-permute-done.q1), channel_id=1, source_target_pairs={{0,16},{16,0},{1,17},{17,1},{2,18},{18,2},{3,19},{19,3},{4,20},{20... | collective-permute-start | bytes 638984 | tf_op jit(solution)/shard_map/ppermute | solution.py:383
  27.4 1.1 %collective-permute-done.2.q3 = bf16[208,512]{1,0:T(8,128)(2,1)S(1)} collective-permute-done((bf16[208,512]{1,0:T(8,128)(2,1)S(1)}, bf16[208,512]{1,0:T(8,128)(2,1)S(1)}, u32[]{:S(2)}, u32[]{:S(2)}) %collective-permute-start.2) | collective-permute-done | bytes 213024 | tf_op jit(solution)/shard_map/ppermute | solution.py:383
  28.4 10.4 %all-to-all-done.kv_ref = bf16[8,400,128]{2,1,0:T(8,128)(2,1)S(1)} async-done(((bf16[8,400,128]{2,1,0:T(8,128)(2,1)}), bf16[8,400,128]{2,1,0:T(8,128)(2,1)S(1)}, u32[]{:S(2)}, u32[]{:S(2)}) %all-to-all-start) | async-done | bytes 819232 | tf_op jit(solution)/shard_map/all_to_all | solution.py:391
  38.9 5.0 %softmax_stats.1 = (f32[4,24,128]{2,1,0:T(8,128)S(1)}, bf16[1536,128]{1,0:T(8,128)(2,1)S(1)}, bf16[1536,128]{1,0:T(8,128)(2,1)S(1)}, bf16[1536,128]{1,0:T(8,128)...) custom-call(bf16[208,512]{1,0:T(8,128)(2,1)S(1)} %rotate_queries.1.q0, ...), custom_call_target="tpu_custom_call" | custom-call | flops 1200000000 | bytes 2000000 | tf_op jit(solution)/shard_map/softmax_stats/pallas_call | solution.py:236
  43.9 5.8 %all_to_all.20.st_ref = f32[4,24,128]{2,1,0:T(8,128)S(1)} all-to-all(f32[4,24,128]{2,1,0:T(8,128)S(1)} %get-tuple-element.21), channel_id=1, replica_groups=mesh['z'=8,'xl'=2,'core'=2,'xh'=2,'yh'=4,'yl'=2] {'xl','core'}, dimensions={0} | all-to-all | bytes 98304 | tf_op jit(solution)/shard_map/all_to_all | solution.py:397
  49.7 7.7 %tile_gradients.1 = (bf16[16,96,256]{2,1,0:T(8,128)(2,1)}, f32[4,96,256]{2,1,0:T(8,128)S(1)}, f32[4,96,256]{2,1,0:T(8,128)S(1)}) custom-call(s32[64]{0:T(128)S(1)} %get-tuple-element.16.perm_ref, bf16[1536,128]{1,0:T(8,128)(2,1)S(1)} %get-tuple-element.17.qs_ref, bf16[1536,128]{1,0:T(8,128)(2,1)S(1)} %get-tuple-element.18.gs_ref, ...), custom_call_target="tpu_custom_call" | custom-call | flops 3000000000 | bytes 3000000 | tf_op jit(solution)/shard_map/tile_gradients/pallas_call | solution.py:319
  57.4 4.8 %all-to-all-start.2 = ((bf16[16,96,256]{2,1,0:T(8,128)(2,1)}), bf16[16,96,256]{2,1,0:T(8,128)(2,1)S(1)}, u32[]{:S(2)}, u32[]{:S(2)}) async-start(bf16[16,96,256]{2,1,0:T(8,128)(2,1)} %get-tuple-element.24), calls=%async_computation.2 | async-start | bytes 1572864 | tf_op jit(solution)/shard_map/all_to_all | solution.py:401
  62.2 2.7 %collective-permute-start.3 = (f32[4,96,256]{2,1,0:T(8,128)S(1)}, f32[4,96,256]{2,1,0:T(8,128)S(1)}, u32[]{:S(2)}, u32[]{:S(2)}) collective-permute-start(f32[4,96,256]{2,1,0:T(8,128)S(1)} %get-tuple-element.23), channel_id=1, source_target_pairs={{0,16},{16,0},{1,17},{17,1},{2,18},{18,2},{3,19},{19,3},{4,20},{20... | collective-permute-start | bytes 1179656 | tf_op jit(solution)/shard_map/ppermute | solution.py:383
  65.0 1.3 %collective-permute-done.3 = f32[4,96,256]{2,1,0:T(8,128)S(1)} collective-permute-done((f32[4,96,256]{2,1,0:T(8,128)S(1)}, f32[4,96,256]{2,1,0:T(8,128)S(1)}, u32[]{:S(2)}, u32[]{:S(2)}) %collective-permute-start.3) | collective-permute-done | bytes 393248 | tf_op jit(solution)/shard_map/ppermute | solution.py:383
  66.4 1.9 %collective-permute-start.4 = (f32[2,96,256]{2,1,0:T(8,128)S(1)}, f32[2,96,256]{2,1,0:T(8,128)S(1)}, u32[]{:S(2)}, u32[]{:S(2)}) collective-permute-start(f32[2,96,256]{2,1,0:T(8,128)S(1)} %get-tuple-element.25), channel_id=1, source_target_pairs={{0,32},{32,0},{1,33},{33,1},{2,34},{34,2},{3,35},{35,3},{4,36},{36... | collective-permute-start | bytes 589832 | tf_op jit(solution)/shard_map/ppermute | solution.py:383
  68.3 14.8 %all-to-all-done.2.parts_ref = bf16[16,96,256]{2,1,0:T(8,128)(2,1)S(1)} async-done(((bf16[16,96,256]{2,1,0:T(8,128)(2,1)}), bf16[16,96,256]{2,1,0:T(8,128)(2,1)S(1)}, u32[]{:S(2)}, u32[]{:S(2)}) %all-to-all-start.2) | async-done | bytes 786464 | tf_op jit(solution)/shard_map/all_to_all | solution.py:401
  83.0 0.8 square_sums.1
  83.9 6.5 %all-to-all-start.3 = ((f32[64,2,128]{2,1,0:T(2,128)}), f32[64,2,128]{2,1,0:T(2,128)S(1)}, u32[]{:S(2)}, u32[]{:S(2)}) async-start(f32[64,2,128]{2,1,0:T(2,128)} %square_sums.1), calls=%async_computation.3 | async-start | bytes 131072 | tf_op jit(solution)/shard_map/all_to_all | solution.py:402
  90.4 0.8 query_gradient.1
  91.1 8.3 %all-to-all-done.3 = f32[64,2,128]{2,1,0:T(2,128)S(1)} async-done(((f32[64,2,128]{2,1,0:T(2,128)}), f32[64,2,128]{2,1,0:T(2,128)S(1)}, u32[]{:S(2)}, u32[]{:S(2)}) %all-to-all-start.3) | async-done | bytes 65568 | tf_op jit(solution)/shard_map/all_to_all | solution.py:402
  99.4 0.1 reduce_sum.9
  99.6 0.5 fusion
  (11 shorter events, 0.1 us)
Async XLA Ops:
  3.6 11.0 %copy-start = (f32[2,192,128]{2,1,0:T(8,128)S(1)}, f32[2,192,128]{2,1,0:T(8,128)}, u32[]{:S(2)}) copy-start(f32[2,192,128]{2,1,0:T(8,128)} %get-tuple-element.14.cs_ref) | copy-start | bytes 589828
  3.6 11.0 %copy-start.1 = (bf16[192,256]{1,0:T(8,128)(2,1)S(1)}, bf16[192,256]{1,0:T(8,128)(2,1)}, u32[]{:S(2)}) copy-start(bf16[192,256]{1,0:T(8,128)(2,1)} %q_ref.1) | copy-start | bytes 294916
  3.6 11.0 %copy-start.2 = (bf16[192,256]{1,0:T(8,128)(2,1)S(1)}, bf16[192,256]{1,0:T(8,128)(2,1)}, u32[]{:S(2)}) copy-start(bf16[192,256]{1,0:T(8,128)(2,1)} %g_ref.1) | copy-start | bytes 294916
  3.6 35.3 %all-to-all-start = ((bf16[8,400,128]{2,1,0:T(8,128)(2,1)}), bf16[8,400,128]{2,1,0:T(8,128)(2,1)S(1)}, u32[]{:S(2)}, u32[]{:S(2)}) async-start(bf16[8,400,128]{2,1,0:T(8,128)(2,1)} %get-tuple-element.15), calls=%async_computation | async-start | bytes 1638400 | tf_op jit(solution)/shard_map/all_to_all | solution.py:391
  14.6 0.7 copy-start.3
  15.9 7.7 %collective-permute-start = (bf16[208,512]{1,0:T(8,128)(2,1)S(1)}, bf16[208,512]{1,0:T(8,128)(2,1)S(1)}, u32[]{:S(2)}, u32[]{:S(2)}) collective-permute-start(bf16[208,512]{1,0:T(8,128)(2,1)S(1)} %rotate_queries.1.q0), channel_id=1, source_target_pairs={{0,32},{32,0},{1,33},{33,1},{2,34},{34,2},{3,35},{35,3},{4,36},{36... | collective-permute-start | bytes 638984 | tf_op jit(solution)/shard_map/ppermute | solution.py:383
  19.0 8.3 %collective-permute-start.1 = (bf16[208,512]{1,0:T(8,128)(2,1)S(1)}, bf16[208,512]{1,0:T(8,128)(2,1)S(1)}, u32[]{:S(2)}, u32[]{:S(2)}) collective-permute-start(bf16[208,512]{1,0:T(8,128)(2,1)S(1)} %rotate_queries.1.q0), channel_id=1, source_target_pairs={{0,16},{16,0},{1,17},{17,1},{2,18},{18,2},{3,19},{19,3},{4,20},{20... | collective-permute-start | bytes 638984 | tf_op jit(solution)/shard_map/ppermute | solution.py:383
  23.6 4.8 %collective-permute-start.2 = (bf16[208,512]{1,0:T(8,128)(2,1)S(1)}, bf16[208,512]{1,0:T(8,128)(2,1)S(1)}, u32[]{:S(2)}, u32[]{:S(2)}) collective-permute-start(bf16[208,512]{1,0:T(8,128)(2,1)S(1)} %collective-permute-done.q1), channel_id=1, source_target_pairs={{0,16},{16,0},{1,17},{17,1},{2,18},{18,2},{3,19},{19,3},{4,20},{20... | collective-permute-start | bytes 638984 | tf_op jit(solution)/shard_map/ppermute | solution.py:383
  57.4 25.6 %all-to-all-start.2 = ((bf16[16,96,256]{2,1,0:T(8,128)(2,1)}), bf16[16,96,256]{2,1,0:T(8,128)(2,1)S(1)}, u32[]{:S(2)}, u32[]{:S(2)}) async-start(bf16[16,96,256]{2,1,0:T(8,128)(2,1)} %get-tuple-element.24), calls=%async_computation.2 | async-start | bytes 1572864 | tf_op jit(solution)/shard_map/all_to_all | solution.py:401
  62.2 4.1 %collective-permute-start.3 = (f32[4,96,256]{2,1,0:T(8,128)S(1)}, f32[4,96,256]{2,1,0:T(8,128)S(1)}, u32[]{:S(2)}, u32[]{:S(2)}) collective-permute-start(f32[4,96,256]{2,1,0:T(8,128)S(1)} %get-tuple-element.23), channel_id=1, source_target_pairs={{0,16},{16,0},{1,17},{17,1},{2,18},{18,2},{3,19},{19,3},{4,20},{20... | collective-permute-start | bytes 1179656 | tf_op jit(solution)/shard_map/ppermute | solution.py:383
  66.4 24.0 %collective-permute-start.4 = (f32[2,96,256]{2,1,0:T(8,128)S(1)}, f32[2,96,256]{2,1,0:T(8,128)S(1)}, u32[]{:S(2)}, u32[]{:S(2)}) collective-permute-start(f32[2,96,256]{2,1,0:T(8,128)S(1)} %get-tuple-element.25), channel_id=1, source_target_pairs={{0,32},{32,0},{1,33},{33,1},{2,34},{34,2},{3,35},{35,3},{4,36},{36... | collective-permute-start | bytes 589832 | tf_op jit(solution)/shard_map/ppermute | solution.py:383
  83.9 15.5 %all-to-all-start.3 = ((f32[64,2,128]{2,1,0:T(2,128)}), f32[64,2,128]{2,1,0:T(2,128)S(1)}, u32[]{:S(2)}, u32[]{:S(2)}) async-start(f32[64,2,128]{2,1,0:T(2,128)} %square_sums.1), calls=%async_computation.3 | async-start | bytes 131072 | tf_op jit(solution)/shard_map/all_to_all | solution.py:402

commit v2 on v1

--- a/solution.py
+++ b/solution.py
@@ -21,7 +21,7 @@
 FLOOR = -1e29
 MIB = 1024 * 1024
 VMEM = 20 * MIB
-VMEM_LARGE = 40 * MIB
+VMEM_LARGE = 32 * MIB
 VMEM_ALL = 60 * MIB
 ROWS = 2 * TOK + 16
 AX_Z, AX_X, AX_C = "z", "xl", "core"
@@ -172,7 +172,7 @@
     return pl.ds(pl.multiple_of(start, BLOCK), count)
 
 
-def stats_kernel(q0, q1, q2, q3, kv_ref, st_ref, qs_ref, gs_ref, ks_ref, vs_ref, perm_ref, m_ref, l_ref, a_ref):
+def sort_kernel(q0, q1, q2, q3, qs_ref, gs_ref, qpos_ref, perm_ref):
     slots = (q0, q1, q2, q3)
     ids = [block_id(ref, j) for ref in slots for j in range(2)]
     for j, r in enumerate(ranks_of(ids)):
@@ -183,6 +183,32 @@
             to = block_rows(r * TOK + head * BLOCK, BLOCK)
             qs_ref[to, :] = ref[rows, head * HD : (head + 1) * HD]
             gs_ref[to, :] = ref[rows, (2 + head) * HD : (3 + head) * HD]
+    qpos_ref[...] = query_positions(perm_ref, 0)
+
+
+def sort_queries(slots):
+    rows = jax.ShapeDtypeStruct((QL, HD), jnp.bfloat16)
+    return pl.pallas_call(
+        sort_kernel,
+        in_specs=[vmem()] * 4,
+        out_specs=[vmem()] * 3 + [smem()],
+        out_shape=[
+            rows,
+            rows,
+            jax.ShapeDtypeStruct((1, QL), jnp.int32),
+            jax.ShapeDtypeStruct((16,), jnp.int32),
+        ],
+        compiler_params=pltpu.CompilerParams(vmem_limit_bytes=VMEM),
+        cost_estimate=pl.CostEstimate(flops=10**6, bytes_accessed=10**6, transcendentals=0),
+        name="sort_queries",
+    )(*slots)
+
+
+def stats_kernel(
+    order_ref, qs_ref, gs_ref, qpos_ref, kv_ref, st_ref, ks_ref, s_ref, d_ref, perm_ref, vs_ref, m_ref, l_ref, a_ref
+):
+    for j in range(16):
+        perm_ref[j] = order_ref[j]
     ids = [x for c in range(NK) for x in key_ids(kv_ref, c)]
     for j, r in enumerate(ranks_of(ids)):
         perm_ref[16 + r] = j
@@ -205,8 +231,9 @@
                 cols = slice(first * QT, QL)
                 s = dot(ks_ref[rows, :], qs_ref[cols, :], 1, 1) * (SCALE * LOG2E)
                 d = dot(vs_ref[rows, :], gs_ref[cols, :], 1, 1)
-                visible = key_positions(perm_ref, pair) <= query_positions(perm_ref, first)
-                s = jnp.where(visible, s, FILL)
+                s = jnp.where(key_positions(perm_ref, pair) <= qpos_ref[:, cols], s, FILL)
+                s_ref[pair, :, cols] = s
+                d_ref[pair, :, cols] = d
                 m = m_ref[:, cols]
                 m2 = jnp.maximum(m, jnp.max(s, axis=0, keepdims=True))
                 p = jnp.exp2(s - m2)
@@ -231,28 +258,27 @@
             st_ref[i, STAT + c : STAT + c + 1, :] = delta
 
 
-def stats(slots, kv):
-    rows = jax.ShapeDtypeStruct((QL, HD), jnp.bfloat16)
+def stats(order, qs, gs, qpos, kv):
+    products = jax.ShapeDtypeStruct((NK, TOK, QL), jnp.float32)
     return pl.pallas_call(
         stats_kernel,
-        in_specs=[vmem()] * 5,
-        out_specs=[vmem()] * 5 + [smem()],
+        in_specs=[smem()] + [vmem()] * 4,
+        out_specs=[vmem()] * 4 + [smem()],
         out_shape=[
             jax.ShapeDtypeStruct((NQ, 2 * STAT, HD), jnp.float32),
-            rows,
-            rows,
-            rows,
-            rows,
+            jax.ShapeDtypeStruct((NK * TOK, HD), jnp.bfloat16),
+            products,
+            products,
             jax.ShapeDtypeStruct((64,), jnp.int32),
         ],
-        scratch_shapes=[pltpu.VMEM((1, QL), jnp.float32)] * 3,
+        scratch_shapes=[pltpu.VMEM((NK * TOK, HD), jnp.bfloat16)] + [pltpu.VMEM((1, QL), jnp.float32)] * 3,
         compiler_params=pltpu.CompilerParams(vmem_limit_bytes=VMEM_LARGE),
         cost_estimate=pl.CostEstimate(flops=12 * 10**8, bytes_accessed=2 * 10**6, transcendentals=24 * 10**5),
         name="softmax_stats",
-    )(*slots, kv)
-
-
-def grad_kernel(perm_ref, qs_ref, gs_ref, ks_ref, vs_ref, st_ref, dkv_ref, keep_ref, send_ref, dqt_ref, lse_ref, delta_ref):
+    )(order, qs, gs, qpos, kv)
+
+
+def grad_kernel(perm_ref, qs_ref, gs_ref, ks_ref, s_ref, d_ref, st_ref, dkv_ref, keep_ref, send_ref, dqt_ref, lse_ref, delta_ref):
     ms = [st_ref[i, :STAT, :] for i in range(NQ)]
     m = functools.reduce(jnp.maximum, ms)
     w = [jnp.exp2(x - m) for x in ms]
@@ -274,12 +300,8 @@
             def _():
                 cols = slice(first * QT, QL)
                 k, q, g = ks_ref[rows, :], qs_ref[cols, :], gs_ref[cols, :]
-                s = dot(k, q, 1, 1) * (SCALE * LOG2E)
-                d = dot(vs_ref[rows, :], g, 1, 1)
-                visible = key_positions(perm_ref, pair) <= query_positions(perm_ref, first)
-                s = jnp.where(visible, s, FILL)
-                p = jnp.exp2(s - lse_ref[:, cols])
-                ds = (p * (d - delta_ref[:, cols])).astype(jnp.bfloat16)
+                p = jnp.exp2(s_ref[pair, :, cols] - lse_ref[:, cols])
+                ds = (p * (d_ref[pair, :, cols] - delta_ref[:, cols])).astype(jnp.bfloat16)
                 dv = dot(p.astype(jnp.bfloat16), g, 1, 0).astype(jnp.bfloat16)
                 dk = dot(ds, q, 1, 0).astype(jnp.bfloat16)
                 dqt_ref[:, cols] += dot(k, ds, 0, 0)
@@ -314,11 +336,11 @@
                 send_ref[block - NQ] = both
 
 
-def grads(perm, qs, gs, ks, vs, st):
+def grads(perm, qs, gs, ks, s, d, st):
     half = jax.ShapeDtypeStruct((NQ, BLOCK, 2 * HD), jnp.float32)
     return pl.pallas_call(
         grad_kernel,
-        in_specs=[smem()] + [vmem()] * 5,
+        in_specs=[smem()] + [vmem()] * 6,
         out_specs=[vmem()] * 3,
         out_shape=[jax.ShapeDtypeStruct((2 * NK, BLOCK, 2 * HD), jnp.bfloat16), half, half],
         scratch_shapes=[
@@ -329,7 +351,7 @@
         compiler_params=pltpu.CompilerParams(vmem_limit_bytes=VMEM_LARGE),
         cost_estimate=pl.CostEstimate(flops=30 * 10**8, bytes_accessed=3 * 10**6, transcendentals=24 * 10**5),
         name="tile_gradients",
-    )(perm, qs, gs, ks, vs, st)
+    )(perm, qs, gs, ks, s, d, st)
 
 
 def dq_kernel(a_ref, b_ref, c_ref, cs_ref, out_ref):
@@ -393,9 +415,10 @@
     other_x = swap(qg, AX_X)
     other_core = swap(qg, AX_C)
     other_both = swap(other_x, AX_C)
-    st, qs, gs, ks, vs, perm = stats((qg, other_x, other_core, other_both), kv_all)
+    qs, gs, qpos, order = sort_queries((qg, other_x, other_core, other_both))
+    st, ks, s, d, perm = stats(order, qs, gs, qpos, kv_all)
     st_all = lax.all_to_all(st, QGROUP, 0, 0)
-    dkv, keep, send = grads(perm, qs, gs, ks, vs, st_all)
+    dkv, keep, send = grads(perm, qs, gs, ks, s, d, st_all)
     near = swap(send, AX_C)
     far = swap(keep[2:] + near[2:], AX_X)
     parts = lax.all_to_all(dkv, KGROUP, 0, 0)

time: 101 us -> 97.8 us (0.968)
  waiting for transfers between devices: 37.3 us -> 33.1 us
  local copies, waits for them, and re-layouts: 1.18 us -> 3.91 us
  Pallas kernels: 17.9 us -> 16.4 us
    all_to_all x1, waiting for transfers between devices: 10.4 us -> 6.78 us  [body(): kv_all = lax.all_to_all(kv, AX_Z, 0, 0)]
    unnamed x8 -> x10, local copies, waits for them, and re-layouts: 0.66 us -> 3.39 us
    pallas_call x2 -> x3, Pallas kernels: 12.8 us -> 11.2 us  [the longest x1 5.27 us: grads(): pl.pallas_call(grad_kernel, in_specs=[smem()] + [vmem()] * 6, out_specs=[...]
  transfers between devices with their start and end apart: 8 -> 8, of which waited for: 6 -> 6; matrix products, arithmetic and copies ran while one was open for 0% -> 0% of each run, Pallas kernels for 2% -> 3%
where the time goes in v2:
time: 97.8 us; the launch traced here: 97.2 us
  starting transfers between devices  36.5 us (37%)
  waiting for transfers between devices  33.1 us (34%)
  Pallas kernels  16.4 us (17%)
  blocking collectives  6.24 us (6%)
  local copies, waits for them, and re-layouts  3.91 us (4%)
    ppermute x5, starting transfers between devices, swap(): return lax.ppermute(value, axis, [(0, 1), (1, 0)])  15 us
    all_to_all x1, waiting for transfers between devices, body(): parts = lax.all_to_all(dkv, KGROUP, 0, 0)  14.3 us
    all_to_all x1, starting transfers between devices, body(): kv_all = lax.all_to_all(kv, AX_Z, 0, 0)  10.9 us
    all_to_all x1, waiting for transfers between devices, body(): sums = lax.all_to_all(squares(yl.reshape(1), parts, cs), ALLGROUP, 0, 0)  8.28 us
    all_to_all x1, starting transfers between devices, body(): sums = lax.all_to_all(squares(yl.reshape(1), parts, cs), ALLGROUP, 0, 0)  6.82 us
    all_to_all x1, waiting for transfers between devices, body(): kv_all = lax.all_to_all(kv, AX_Z, 0, 0)  6.78 us
    all_to_all x1, blocking collectives, body(): st_all = lax.all_to_all(st, QGROUP, 0, 0)  6.24 us
    pallas_call x1, Pallas kernels, grads(): pl.pallas_call(grad_kernel, in_specs=[smem()] + [vmem()] * 6, out_specs=[...  5.27 us
  transfers between devices with their start and end apart: 8, of which 6 were waited for; matrix products, arithmetic and copies ran while one was open for 0% of the time, Pallas kernels for 3%

profile of v2, /device:TPU:1, one launch (start us, length us, event | category | flops | bytes accessed | tf_op | source)
XLA Modules:
  0.0 97.2 jit_solution(12266538353976569983)
XLA Ops:
  0.6 2.9 %rotate_keys.1 = (bf16[8,400,128]{2,1,0:T(8,128)(2,1)}, f32[2,192,128]{2,1,0:T(8,128)}) custom-call(s32[1]{0:T(128)} %bitcast.kvi_ref, s32[192]{0:T(256)} %pos_ref.3, f32[1,128]{1,0:T(1,128)} %constant.26.clone.freq_ref, bf16[192,1024]{1,0:T(8,128)(2,1)} %k_ref.1, bf16[192,1024]{1,0:T(8,128)(2,1)} %v_ref.1), custom_call_target="tpu_custom_call" | custom-call | flops 1000000 | bytes 1000000 | tf_op jit(solution)/shard_map/rotate_keys/pallas_call | solution.py:94
  3.6 10.9 %all-to-all-start = ((bf16[8,400,128]{2,1,0:T(8,128)(2,1)}), bf16[8,400,128]{2,1,0:T(8,128)(2,1)S(1)}, u32[]{:S(2)}, u32[]{:S(2)}) async-start(bf16[8,400,128]{2,1,0:T(8,128)(2,1)} %get-tuple-element.22), calls=%async_computation | async-start | bytes 1638400 | tf_op jit(solution)/shard_map/all_to_all | solution.py:413
  14.4 0.9 copy-done
  15.4 0.9 copy-done.2
  16.3 0.9 copy-done.3
  18.5 3.1 %collective-permute-start = (bf16[208,512]{1,0:T(8,128)(2,1)S(1)}, bf16[208,512]{1,0:T(8,128)(2,1)S(1)}, u32[]{:S(2)}, u32[]{:S(2)}) collective-permute-start(bf16[208,512]{1,0:T(8,128)(2,1)S(1)} %rotate_queries.1.q0), channel_id=1, source_target_pairs={{0,32},{32,0},{1,33},{33,1},{2,34},{34,2},{3,35},{35,3},{4,36},{36... | collective-permute-start | bytes 638984 | tf_op jit(solution)/shard_map/ppermute | solution.py:405
  21.6 3.1 %collective-permute-start.1 = (bf16[208,512]{1,0:T(8,128)(2,1)S(1)}, bf16[208,512]{1,0:T(8,128)(2,1)S(1)}, u32[]{:S(2)}, u32[]{:S(2)}) collective-permute-start(bf16[208,512]{1,0:T(8,128)(2,1)S(1)} %rotate_queries.1.q0), channel_id=1, source_target_pairs={{0,16},{16,0},{1,17},{17,1},{2,18},{18,2},{3,19},{19,3},{4,20},{20... | collective-permute-start | bytes 638984 | tf_op jit(solution)/shard_map/ppermute | solution.py:405
  24.8 1.4 %collective-permute-done.q1 = bf16[208,512]{1,0:T(8,128)(2,1)S(1)} collective-permute-done((bf16[208,512]{1,0:T(8,128)(2,1)S(1)}, bf16[208,512]{1,0:T(8,128)(2,1)S(1)}, u32[]{:S(2)}, u32[]{:S(2)}) %collective-permute-start) | collective-permute-done | bytes 213024 | tf_op jit(solution)/shard_map/ppermute | solution.py:405
  26.2 3.8 %collective-permute-start.2 = (bf16[208,512]{1,0:T(8,128)(2,1)S(1)}, bf16[208,512]{1,0:T(8,128)(2,1)S(1)}, u32[]{:S(2)}, u32[]{:S(2)}) collective-permute-start(bf16[208,512]{1,0:T(8,128)(2,1)S(1)} %collective-permute-done.q1), channel_id=1, source_target_pairs={{0,16},{16,0},{1,17},{17,1},{2,18},{18,2},{3,19},{19,3},{4,20},{20... | collective-permute-start | bytes 638984 | tf_op jit(solution)/shard_map/ppermute | solution.py:405
  29.9 1.1 %collective-permute-done.2.q3 = bf16[208,512]{1,0:T(8,128)(2,1)S(1)} collective-permute-done((bf16[208,512]{1,0:T(8,128)(2,1)S(1)}, bf16[208,512]{1,0:T(8,128)(2,1)S(1)}, u32[]{:S(2)}, u32[]{:S(2)}) %collective-permute-start.2) | collective-permute-done | bytes 213024 | tf_op jit(solution)/shard_map/ppermute | solution.py:405
  31.0 0.9 sort_queries.1
  31.9 6.8 %all-to-all-done.kv_ref = bf16[8,400,128]{2,1,0:T(8,128)(2,1)S(1)} async-done(((bf16[8,400,128]{2,1,0:T(8,128)(2,1)}), bf16[8,400,128]{2,1,0:T(8,128)(2,1)S(1)}, u32[]{:S(2)}, u32[]{:S(2)}) %all-to-all-start) | async-done | bytes 819232 | tf_op jit(solution)/shard_map/all_to_all | solution.py:413
  38.7 5.1 %softmax_stats.1 = (f32[4,24,128]{2,1,0:T(8,128)S(1)}, bf16[1536,128]{1,0:T(8,128)(2,1)S(1)}, f32[8,192,1536]{2,1,0:T(8,128)S(1)}, f32[8,192,1536]{2,1,0:T(8,128)S(1)}, s32[64]{0:T(128)S(1)}) custom-call(s32[16]{0:T(128)S(1)} %get-tuple-element.18.order_ref, bf16[1536,128]{1,0:T(8,128)(2,1)S(1)} %get-tuple-element.19.qs_ref, ...), custom_call_target="tpu_custom_call" | custom-call | flops 1200000000 | bytes 2000000 | tf_op jit(solution)/shard_map/softmax_stats/pallas_call | solution.py:263
  43.8 6.2 %all_to_all.20.st_ref = f32[4,24,128]{2,1,0:T(8,128)S(1)} all-to-all(f32[4,24,128]{2,1,0:T(8,128)S(1)} %get-tuple-element.27), channel_id=1, replica_groups=mesh['z'=8,'xl'=2,'core'=2,'xh'=2,'yh'=4,'yl'=2] {'xl','core'}, dimensions={0} | all-to-all | bytes 98304 | tf_op jit(solution)/shard_map/all_to_all | solution.py:420
  50.0 5.3 %tile_gradients.1 = (bf16[16,96,256]{2,1,0:T(8,128)(2,1)}, f32[4,96,256]{2,1,0:T(8,128)S(1)}, f32[4,96,256]{2,1,0:T(8,128)S(1)}) custom-call(s32[64]{0:T(128)S(1)} %get-tuple-element.23.perm_ref, bf16[1536,128]{1,0:T(8,128)(2,1)S(1)} %get-tuple-element.19.qs_ref, bf16[1536,128]{1,0:T(8,128)(2,1)S(1)} %get-tuple-element.20.gs_ref, ...), custom_call_target="tpu_custom_call" | custom-call | flops 3000000000 | bytes 3000000 | tf_op jit(solution)/shard_map/tile_gradients/pallas_call | solution.py:341
  55.3 3.8 %all-to-all-start.2 = ((bf16[16,96,256]{2,1,0:T(8,128)(2,1)}), bf16[16,96,256]{2,1,0:T(8,128)(2,1)S(1)}, u32[]{:S(2)}, u32[]{:S(2)}) async-start(bf16[16,96,256]{2,1,0:T(8,128)(2,1)} %get-tuple-element.30), calls=%async_computation.2 | async-start | bytes 1572864 | tf_op jit(solution)/shard_map/all_to_all | solution.py:424
  59.1 3.1 %collective-permute-start.3 = (f32[4,96,256]{2,1,0:T(8,128)S(1)}, f32[4,96,256]{2,1,0:T(8,128)S(1)}, u32[]{:S(2)}, u32[]{:S(2)}) collective-permute-start(f32[4,96,256]{2,1,0:T(8,128)S(1)} %get-tuple-element.29), channel_id=1, source_target_pairs={{0,16},{16,0},{1,17},{17,1},{2,18},{18,2},{3,19},{19,3},{4,20},{20... | collective-permute-start | bytes 1179656 | tf_op jit(solution)/shard_map/ppermute | solution.py:405
  62.2 1.3 %collective-permute-done.3 = f32[4,96,256]{2,1,0:T(8,128)S(1)} collective-permute-done((f32[4,96,256]{2,1,0:T(8,128)S(1)}, f32[4,96,256]{2,1,0:T(8,128)S(1)}, u32[]{:S(2)}, u32[]{:S(2)}) %collective-permute-start.3) | collective-permute-done | bytes 393248 | tf_op jit(solution)/shard_map/ppermute | solution.py:405
  63.6 1.9 %collective-permute-start.4 = (f32[2,96,256]{2,1,0:T(8,128)S(1)}, f32[2,96,256]{2,1,0:T(8,128)S(1)}, u32[]{:S(2)}, u32[]{:S(2)}) collective-permute-start(f32[2,96,256]{2,1,0:T(8,128)S(1)} %get-tuple-element.31), channel_id=1, source_target_pairs={{0,32},{32,0},{1,33},{33,1},{2,34},{34,2},{3,35},{35,3},{4,36},{36... | collective-permute-start | bytes 589832 | tf_op jit(solution)/shard_map/ppermute | solution.py:405
  65.5 14.3 %all-to-all-done.2.parts_ref = bf16[16,96,256]{2,1,0:T(8,128)(2,1)S(1)} async-done(((bf16[16,96,256]{2,1,0:T(8,128)(2,1)}), bf16[16,96,256]{2,1,0:T(8,128)(2,1)S(1)}, u32[]{:S(2)}, u32[]{:S(2)}) %all-to-all-start.2) | async-done | bytes 786464 | tf_op jit(solution)/shard_map/all_to_all | solution.py:424
  79.8 0.8 square_sums.1
  80.6 6.8 %all-to-all-start.3 = ((f32[64,2,128]{2,1,0:T(2,128)}), f32[64,2,128]{2,1,0:T(2,128)S(1)}, u32[]{:S(2)}, u32[]{:S(2)}) async-start(f32[64,2,128]{2,1,0:T(2,128)} %square_sums.1), calls=%async_computation.3 | async-start | bytes 131072 | tf_op jit(solution)/shard_map/all_to_all | solution.py:425
  87.4 0.8 query_gradient.1
  88.2 8.3 %all-to-all-done.3 = f32[64,2,128]{2,1,0:T(2,128)S(1)} async-done(((f32[64,2,128]{2,1,0:T(2,128)}), f32[64,2,128]{2,1,0:T(2,128)S(1)}, u32[]{:S(2)}, u32[]{:S(2)}) %all-to-all-start.3) | async-done | bytes 65568 | tf_op jit(solution)/shard_map/all_to_all | solution.py:425
  (14 shorter events, 2.1 us)
Async XLA Ops:
  3.6 35.1 %all-to-all-start = ((bf16[8,400,128]{2,1,0:T(8,128)(2,1)}), bf16[8,400,128]{2,1,0:T(8,128)(2,1)S(1)}, u32[]{:S(2)}, u32[]{:S(2)}) async-start(bf16[8,400,128]{2,1,0:T(8,128)(2,1)} %get-tuple-element.22), calls=%async_computation | async-start | bytes 1638400 | tf_op jit(solution)/shard_map/all_to_all | solution.py:413
  14.4 0.9 copy-start
  15.4 0.9 copy-start.2
  16.2 0.9 copy-start.3
  17.1 0.7 copy-start.4
  18.5 7.7 %collective-permute-start = (bf16[208,512]{1,0:T(8,128)(2,1)S(1)}, bf16[208,512]{1,0:T(8,128)(2,1)S(1)}, u32[]{:S(2)}, u32[]{:S(2)}) collective-permute-start(bf16[208,512]{1,0:T(8,128)(2,1)S(1)} %rotate_queries.1.q0), channel_id=1, source_target_pairs={{0,32},{32,0},{1,33},{33,1},{2,34},{34,2},{3,35},{35,3},{4,36},{36... | collective-permute-start | bytes 638984 | tf_op jit(solution)/shard_map/ppermute | solution.py:405
  21.6 8.3 %collective-permute-start.1 = (bf16[208,512]{1,0:T(8,128)(2,1)S(1)}, bf16[208,512]{1,0:T(8,128)(2,1)S(1)}, u32[]{:S(2)}, u32[]{:S(2)}) collective-permute-start(bf16[208,512]{1,0:T(8,128)(2,1)S(1)} %rotate_queries.1.q0), channel_id=1, source_target_pairs={{0,16},{16,0},{1,17},{17,1},{2,18},{18,2},{3,19},{19,3},{4,20},{20... | collective-permute-start | bytes 638984 | tf_op jit(solution)/shard_map/ppermute | solution.py:405
  26.2 4.8 %collective-permute-start.2 = (bf16[208,512]{1,0:T(8,128)(2,1)S(1)}, bf16[208,512]{1,0:T(8,128)(2,1)S(1)}, u32[]{:S(2)}, u32[]{:S(2)}) collective-permute-start(bf16[208,512]{1,0:T(8,128)(2,1)S(1)} %collective-permute-done.q1), channel_id=1, source_target_pairs={{0,16},{16,0},{1,17},{17,1},{2,18},{18,2},{3,19},{19,3},{4,20},{20... | collective-permute-start | bytes 638984 | tf_op jit(solution)/shard_map/ppermute | solution.py:405
  50.0 29.8 %copy-start.1 = (f32[2,192,128]{2,1,0:T(8,128)S(1)}, f32[2,192,128]{2,1,0:T(8,128)}, u32[]{:S(2)}) copy-start(f32[2,192,128]{2,1,0:T(8,128)} %get-tuple-element.17.cs_ref) | copy-start | bytes 589828
  55.3 24.5 %all-to-all-start.2 = ((bf16[16,96,256]{2,1,0:T(8,128)(2,1)}), bf16[16,96,256]{2,1,0:T(8,128)(2,1)S(1)}, u32[]{:S(2)}, u32[]{:S(2)}) async-start(bf16[16,96,256]{2,1,0:T(8,128)(2,1)} %get-tuple-element.30), calls=%async_computation.2 | async-start | bytes 1572864 | tf_op jit(solution)/shard_map/all_to_all | solution.py:424
  59.1 4.4 %collective-permute-start.3 = (f32[4,96,256]{2,1,0:T(8,128)S(1)}, f32[4,96,256]{2,1,0:T(8,128)S(1)}, u32[]{:S(2)}, u32[]{:S(2)}) collective-permute-start(f32[4,96,256]{2,1,0:T(8,128)S(1)} %get-tuple-element.29), channel_id=1, source_target_pairs={{0,16},{16,0},{1,17},{17,1},{2,18},{18,2},{3,19},{19,3},{4,20},{20... | collective-permute-start | bytes 1179656 | tf_op jit(solution)/shard_map/ppermute | solution.py:405
  63.6 23.9 %collective-permute-start.4 = (f32[2,96,256]{2,1,0:T(8,128)S(1)}, f32[2,96,256]{2,1,0:T(8,128)S(1)}, u32[]{:S(2)}, u32[]{:S(2)}) collective-permute-start(f32[2,96,256]{2,1,0:T(8,128)S(1)} %get-tuple-element.31), channel_id=1, source_target_pairs={{0,32},{32,0},{1,33},{33,1},{2,34},{34,2},{3,35},{35,3},{4,36},{36... | collective-permute-start | bytes 589832 | tf_op jit(solution)/shard_map/ppermute | solution.py:405
  80.6 15.9 %all-to-all-start.3 = ((f32[64,2,128]{2,1,0:T(2,128)}), f32[64,2,128]{2,1,0:T(2,128)S(1)}, u32[]{:S(2)}, u32[]{:S(2)}) async-start(f32[64,2,128]{2,1,0:T(2,128)} %square_sums.1), calls=%async_computation.3 | async-start | bytes 131072 | tf_op jit(solution)/shard_map/all_to_all | solution.py:425

commit v3 on v2

--- a/solution.py
+++ b/solution.py
@@ -23,6 +23,7 @@
 VMEM = 20 * MIB
 VMEM_LARGE = 32 * MIB
 VMEM_ALL = 60 * MIB
+VMEM_GRADS = 32 * MIB
 ROWS = 2 * TOK + 16
 AX_Z, AX_X, AX_C = "z", "xl", "core"
 QGROUP = (AX_X, AX_C)
@@ -69,15 +70,19 @@
 
 
 def key_kernel(kvi_ref, pos_ref, freq_ref, k_ref, v_ref, kv_ref, cs_ref):
-    row = lax.broadcasted_iota(jnp.int32, (TOK, HD), 0)
-    pos = jnp.where(row < BLOCK, pos_ref[0] + row, pos_ref[BLOCK] + row - BLOCK)
-    angle = pos.astype(jnp.float32) * freq_ref[...]
-    cosine = jnp.cos(angle)
-    lane = lax.broadcasted_iota(jnp.int32, (TOK, HD), 1)
-    sine = jnp.sin(angle)
-    sine = jnp.where(lane < HD // 2, -sine, sine)
-    cs_ref[0] = cosine
-    cs_ref[1] = sine
+    row = lax.broadcasted_iota(jnp.int32, (BLOCK, HD), 0)
+    lane = lax.broadcasted_iota(jnp.int32, (BLOCK, HD), 1)
+    lower = lane < HD // 2
+    angle = (row + jnp.where(lower, pos_ref[0], pos_ref[BLOCK])).astype(jnp.float32) * freq_ref[...]
+
+    def spread(packed):
+        other = pltpu.roll(packed, HD // 2, 1)
+        return jnp.where(lower, packed, other), jnp.where(lower, other, packed)
+
+    for j, (c, s) in enumerate(zip(spread(jnp.cos(angle)), spread(jnp.sin(angle)))):
+        cs_ref[0, j * BLOCK : (j + 1) * BLOCK, :] = c
+        cs_ref[1, j * BLOCK : (j + 1) * BLOCK, :] = jnp.where(lower, -s, s)
+    cosine, sine = cs_ref[0], cs_ref[1]
     key = rotate(k_ref[...], cosine, sine)
     lanes = lax.broadcasted_iota(jnp.int32, (ROWS - 2 * TOK, HD), 1)
     first, second = (lax.div(pos_ref[j * BLOCK], BLOCK) for j in range(2))
@@ -348,7 +353,7 @@
             pltpu.VMEM((1, QL), jnp.float32),
             pltpu.VMEM((1, QL), jnp.float32),
         ],
-        compiler_params=pltpu.CompilerParams(vmem_limit_bytes=VMEM_LARGE),
+        compiler_params=pltpu.CompilerParams(vmem_limit_bytes=VMEM_GRADS),
         cost_estimate=pl.CostEstimate(flops=30 * 10**8, bytes_accessed=3 * 10**6, transcendentals=24 * 10**5),
         name="tile_gradients",
     )(perm, qs, gs, ks, s, d, st)

time: 97.8 us -> 98.6 us (level)
  no operation moved by 1% of the time
where the time goes in v3:
time: 98.6 us; the launch traced here: 97.8 us
  starting transfers between devices  36.2 us (37%)
  waiting for transfers between devices  33.6 us (34%)
  Pallas kernels  17.1 us (17%)
  blocking collectives  6.09 us (6%)
  local copies, waits for them, and re-layouts  3.91 us (4%)
    all_to_all x1, waiting for transfers between devices, body(): parts = lax.all_to_all(dkv, KGROUP, 0, 0)  14.7 us
    ppermute x5, starting transfers between devices, swap(): return lax.ppermute(value, axis, [(0, 1), (1, 0)])  14.7 us
    all_to_all x1, starting transfers between devices, body(): kv_all = lax.all_to_all(kv, AX_Z, 0, 0)  10.9 us
    all_to_all x1, waiting for transfers between devices, body(): sums = lax.all_to_all(squares(yl.reshape(1), parts, cs), ALLGROUP, 0, 0)  8.28 us
    all_to_all x1, waiting for transfers between devices, body(): kv_all = lax.all_to_all(kv, AX_Z, 0, 0)  6.78 us
    all_to_all x1, starting transfers between devices, body(): sums = lax.all_to_all(squares(yl.reshape(1), parts, cs), ALLGROUP, 0, 0)  6.54 us
    all_to_all x1, blocking collectives, body(): st_all = lax.all_to_all(st, QGROUP, 0, 0)  6.09 us
    pallas_call x1, Pallas kernels, grads(): pl.pallas_call(grad_kernel, in_specs=[smem()] + [vmem()] * 6, out_specs=[...  5.78 us
  transfers between devices with their start and end apart: 8, of which 6 were waited for; matrix products, arithmetic and copies ran while one was open for 0% of the time, Pallas kernels for 3%

profile of v3, /device:TPU:1, one launch (start us, length us, event | category | flops | bytes accessed | tf_op | source)
XLA Modules:
  0.0 97.8 jit_solution(17694481369120360333)
XLA Ops:
  0.6 2.8 %rotate_keys.1 = (bf16[8,400,128]{2,1,0:T(8,128)(2,1)}, f32[2,192,128]{2,1,0:T(8,128)}) custom-call(s32[1]{0:T(128)} %bitcast.kvi_ref, s32[192]{0:T(256)} %pos_ref.3, f32[1,128]{1,0:T(1,128)} %constant.26.clone.freq_ref, bf16[192,1024]{1,0:T(8,128)(2,1)} %k_ref.1, bf16[192,1024]{1,0:T(8,128)(2,1)} %v_ref.1), custom_call_target="tpu_custom_call" | custom-call | flops 1000000 | bytes 1000000 | tf_op jit(solution)/shard_map/rotate_keys/pallas_call | solution.py:99
  3.4 10.9 %all-to-all-start = ((bf16[8,400,128]{2,1,0:T(8,128)(2,1)}), bf16[8,400,128]{2,1,0:T(8,128)(2,1)S(1)}, u32[]{:S(2)}, u32[]{:S(2)}) async-start(bf16[8,400,128]{2,1,0:T(8,128)(2,1)} %get-tuple-element.22), calls=%async_computation | async-start | bytes 1638400 | tf_op jit(solution)/shard_map/all_to_all | solution.py:418
  14.3 0.9 copy-done
  15.2 0.9 copy-done.2
  16.1 0.9 copy-done.3
  18.3 3.1 %collective-permute-start = (bf16[208,512]{1,0:T(8,128)(2,1)S(1)}, bf16[208,512]{1,0:T(8,128)(2,1)S(1)}, u32[]{:S(2)}, u32[]{:S(2)}) collective-permute-start(bf16[208,512]{1,0:T(8,128)(2,1)S(1)} %rotate_queries.1.q0), channel_id=1, source_target_pairs={{0,32},{32,0},{1,33},{33,1},{2,34},{34,2},{3,35},{35,3},{4,36},{36... | collective-permute-start | bytes 638984 | tf_op jit(solution)/shard_map/ppermute | solution.py:410
  21.5 3.1 %collective-permute-start.1 = (bf16[208,512]{1,0:T(8,128)(2,1)S(1)}, bf16[208,512]{1,0:T(8,128)(2,1)S(1)}, u32[]{:S(2)}, u32[]{:S(2)}) collective-permute-start(bf16[208,512]{1,0:T(8,128)(2,1)S(1)} %rotate_queries.1.q0), channel_id=1, source_target_pairs={{0,16},{16,0},{1,17},{17,1},{2,18},{18,2},{3,19},{19,3},{4,20},{20... | collective-permute-start | bytes 638984 | tf_op jit(solution)/shard_map/ppermute | solution.py:410
  24.6 1.4 %collective-permute-done.q1 = bf16[208,512]{1,0:T(8,128)(2,1)S(1)} collective-permute-done((bf16[208,512]{1,0:T(8,128)(2,1)S(1)}, bf16[208,512]{1,0:T(8,128)(2,1)S(1)}, u32[]{:S(2)}, u32[]{:S(2)}) %collective-permute-start) | collective-permute-done | bytes 213024 | tf_op jit(solution)/shard_map/ppermute | solution.py:410
  26.0 3.8 %collective-permute-start.2 = (bf16[208,512]{1,0:T(8,128)(2,1)S(1)}, bf16[208,512]{1,0:T(8,128)(2,1)S(1)}, u32[]{:S(2)}, u32[]{:S(2)}) collective-permute-start(bf16[208,512]{1,0:T(8,128)(2,1)S(1)} %collective-permute-done.q1), channel_id=1, source_target_pairs={{0,16},{16,0},{1,17},{17,1},{2,18},{18,2},{3,19},{19,3},{4,20},{20... | collective-permute-start | bytes 638984 | tf_op jit(solution)/shard_map/ppermute | solution.py:410
  29.8 1.1 %collective-permute-done.2.q3 = bf16[208,512]{1,0:T(8,128)(2,1)S(1)} collective-permute-done((bf16[208,512]{1,0:T(8,128)(2,1)S(1)}, bf16[208,512]{1,0:T(8,128)(2,1)S(1)}, u32[]{:S(2)}, u32[]{:S(2)}) %collective-permute-start.2) | collective-permute-done | bytes 213024 | tf_op jit(solution)/shard_map/ppermute | solution.py:410
  30.9 0.9 sort_queries.1
  31.8 6.8 %all-to-all-done.kv_ref = bf16[8,400,128]{2,1,0:T(8,128)(2,1)S(1)} async-done(((bf16[8,400,128]{2,1,0:T(8,128)(2,1)}), bf16[8,400,128]{2,1,0:T(8,128)(2,1)S(1)}, u32[]{:S(2)}, u32[]{:S(2)}) %all-to-all-start) | async-done | bytes 819232 | tf_op jit(solution)/shard_map/all_to_all | solution.py:418
  38.6 5.4 %softmax_stats.1 = (f32[4,24,128]{2,1,0:T(8,128)S(1)}, bf16[1536,128]{1,0:T(8,128)(2,1)S(1)}, f32[8,192,1536]{2,1,0:T(8,128)S(1)}, f32[8,192,1536]{2,1,0:T(8,128)S(1)}, s32[64]{0:T(128)S(1)}) custom-call(s32[16]{0:T(128)S(1)} %get-tuple-element.18.order_ref, bf16[1536,128]{1,0:T(8,128)(2,1)S(1)} %get-tuple-element.19.qs_ref, ...), custom_call_target="tpu_custom_call" | custom-call | flops 1200000000 | bytes 2000000 | tf_op jit(solution)/shard_map/softmax_stats/pallas_call | solution.py:268
  44.0 6.1 %all_to_all.20.st_ref = f32[4,24,128]{2,1,0:T(8,128)S(1)} all-to-all(f32[4,24,128]{2,1,0:T(8,128)S(1)} %get-tuple-element.27), channel_id=1, replica_groups=mesh['z'=8,'xl'=2,'core'=2,'xh'=2,'yh'=4,'yl'=2] {'xl','core'}, dimensions={0} | all-to-all | bytes 98304 | tf_op jit(solution)/shard_map/all_to_all | solution.py:425
  50.1 5.8 %tile_gradients.1 = (bf16[16,96,256]{2,1,0:T(8,128)(2,1)}, f32[4,96,256]{2,1,0:T(8,128)S(1)}, f32[4,96,256]{2,1,0:T(8,128)S(1)}) custom-call(s32[64]{0:T(128)S(1)} %get-tuple-element.23.perm_ref, bf16[1536,128]{1,0:T(8,128)(2,1)S(1)} %get-tuple-element.19.qs_ref, bf16[1536,128]{1,0:T(8,128)(2,1)S(1)} %get-tuple-element.20.gs_ref, ...), custom_call_target="tpu_custom_call" | custom-call | flops 3000000000 | bytes 3000000 | tf_op jit(solution)/shard_map/tile_gradients/pallas_call | solution.py:346
  55.8 4.1 %all-to-all-start.2 = ((bf16[16,96,256]{2,1,0:T(8,128)(2,1)}), bf16[16,96,256]{2,1,0:T(8,128)(2,1)S(1)}, u32[]{:S(2)}, u32[]{:S(2)}) async-start(bf16[16,96,256]{2,1,0:T(8,128)(2,1)} %get-tuple-element.30), calls=%async_computation.2 | async-start | bytes 1572864 | tf_op jit(solution)/shard_map/all_to_all | solution.py:429
  59.9 2.4 %collective-permute-start.3 = (f32[4,96,256]{2,1,0:T(8,128)S(1)}, f32[4,96,256]{2,1,0:T(8,128)S(1)}, u32[]{:S(2)}, u32[]{:S(2)}) collective-permute-start(f32[4,96,256]{2,1,0:T(8,128)S(1)} %get-tuple-element.29), channel_id=1, source_target_pairs={{0,16},{16,0},{1,17},{17,1},{2,18},{18,2},{3,19},{19,3},{4,20},{20... | collective-permute-start | bytes 1179656 | tf_op jit(solution)/shard_map/ppermute | solution.py:410
  62.3 1.3 %collective-permute-done.3 = f32[4,96,256]{2,1,0:T(8,128)S(1)} collective-permute-done((f32[4,96,256]{2,1,0:T(8,128)S(1)}, f32[4,96,256]{2,1,0:T(8,128)S(1)}, u32[]{:S(2)}, u32[]{:S(2)}) %collective-permute-start.3) | collective-permute-done | bytes 393248 | tf_op jit(solution)/shard_map/ppermute | solution.py:410
  63.7 2.2 %collective-permute-start.4 = (f32[2,96,256]{2,1,0:T(8,128)S(1)}, f32[2,96,256]{2,1,0:T(8,128)S(1)}, u32[]{:S(2)}, u32[]{:S(2)}) collective-permute-start(f32[2,96,256]{2,1,0:T(8,128)S(1)} %get-tuple-element.31), channel_id=1, source_target_pairs={{0,32},{32,0},{1,33},{33,1},{2,34},{34,2},{3,35},{35,3},{4,36},{36... | collective-permute-start | bytes 589832 | tf_op jit(solution)/shard_map/ppermute | solution.py:410
  66.0 14.7 %all-to-all-done.2.parts_ref = bf16[16,96,256]{2,1,0:T(8,128)(2,1)S(1)} async-done(((bf16[16,96,256]{2,1,0:T(8,128)(2,1)}), bf16[16,96,256]{2,1,0:T(8,128)(2,1)S(1)}, u32[]{:S(2)}, u32[]{:S(2)}) %all-to-all-start.2) | async-done | bytes 786464 | tf_op jit(solution)/shard_map/all_to_all | solution.py:429
  80.7 0.8 square_sums.1
  81.5 6.5 %all-to-all-start.3 = ((f32[64,2,128]{2,1,0:T(2,128)}), f32[64,2,128]{2,1,0:T(2,128)S(1)}, u32[]{:S(2)}, u32[]{:S(2)}) async-start(f32[64,2,128]{2,1,0:T(2,128)} %square_sums.1), calls=%async_computation.3 | async-start | bytes 131072 | tf_op jit(solution)/shard_map/all_to_all | solution.py:430
  88.1 0.8 query_gradient.1
  88.8 8.3 %all-to-all-done.3 = f32[64,2,128]{2,1,0:T(2,128)S(1)} async-done(((f32[64,2,128]{2,1,0:T(2,128)}), f32[64,2,128]{2,1,0:T(2,128)S(1)}, u32[]{:S(2)}, u32[]{:S(2)}) %all-to-all-start.3) | async-done | bytes 65568 | tf_op jit(solution)/shard_map/all_to_all | solution.py:430
  (14 shorter events, 2.1 us)
Async XLA Ops:
  3.4 35.1 %all-to-all-start = ((bf16[8,400,128]{2,1,0:T(8,128)(2,1)}), bf16[8,400,128]{2,1,0:T(8,128)(2,1)S(1)}, u32[]{:S(2)}, u32[]{:S(2)}) async-start(bf16[8,400,128]{2,1,0:T(8,128)(2,1)} %get-tuple-element.22), calls=%async_computation | async-start | bytes 1638400 | tf_op jit(solution)/shard_map/all_to_all | solution.py:418
  14.3 0.9 copy-start
  15.2 0.9 copy-start.2
  16.1 0.9 copy-start.3
  17.0 0.7 copy-start.4
  18.3 7.7 %collective-permute-start = (bf16[208,512]{1,0:T(8,128)(2,1)S(1)}, bf16[208,512]{1,0:T(8,128)(2,1)S(1)}, u32[]{:S(2)}, u32[]{:S(2)}) collective-permute-start(bf16[208,512]{1,0:T(8,128)(2,1)S(1)} %rotate_queries.1.q0), channel_id=1, source_target_pairs={{0,32},{32,0},{1,33},{33,1},{2,34},{34,2},{3,35},{35,3},{4,36},{36... | collective-permute-start | bytes 638984 | tf_op jit(solution)/shard_map/ppermute | solution.py:410
  21.5 8.3 %collective-permute-start.1 = (bf16[208,512]{1,0:T(8,128)(2,1)S(1)}, bf16[208,512]{1,0:T(8,128)(2,1)S(1)}, u32[]{:S(2)}, u32[]{:S(2)}) collective-permute-start(bf16[208,512]{1,0:T(8,128)(2,1)S(1)} %rotate_queries.1.q0), channel_id=1, source_target_pairs={{0,16},{16,0},{1,17},{17,1},{2,18},{18,2},{3,19},{19,3},{4,20},{20... | collective-permute-start | bytes 638984 | tf_op jit(solution)/shard_map/ppermute | solution.py:410
  26.0 4.8 %collective-permute-start.2 = (bf16[208,512]{1,0:T(8,128)(2,1)S(1)}, bf16[208,512]{1,0:T(8,128)(2,1)S(1)}, u32[]{:S(2)}, u32[]{:S(2)}) collective-permute-start(bf16[208,512]{1,0:T(8,128)(2,1)S(1)} %collective-permute-done.q1), channel_id=1, source_target_pairs={{0,16},{16,0},{1,17},{17,1},{2,18},{18,2},{3,19},{19,3},{4,20},{20... | collective-permute-start | bytes 638984 | tf_op jit(solution)/shard_map/ppermute | solution.py:410
  50.1 30.6 %copy-start.1 = (f32[2,192,128]{2,1,0:T(8,128)S(1)}, f32[2,192,128]{2,1,0:T(8,128)}, u32[]{:S(2)}) copy-start(f32[2,192,128]{2,1,0:T(8,128)} %get-tuple-element.17.cs_ref) | copy-start | bytes 589828
  55.8 24.8 %all-to-all-start.2 = ((bf16[16,96,256]{2,1,0:T(8,128)(2,1)}), bf16[16,96,256]{2,1,0:T(8,128)(2,1)S(1)}, u32[]{:S(2)}, u32[]{:S(2)}) async-start(bf16[16,96,256]{2,1,0:T(8,128)(2,1)} %get-tuple-element.30), calls=%async_computation.2 | async-start | bytes 1572864 | tf_op jit(solution)/shard_map/all_to_all | solution.py:429
  59.9 3.7 %collective-permute-start.3 = (f32[4,96,256]{2,1,0:T(8,128)S(1)}, f32[4,96,256]{2,1,0:T(8,128)S(1)}, u32[]{:S(2)}, u32[]{:S(2)}) collective-permute-start(f32[4,96,256]{2,1,0:T(8,128)S(1)} %get-tuple-element.29), channel_id=1, source_target_pairs={{0,16},{16,0},{1,17},{17,1},{2,18},{18,2},{3,19},{19,3},{4,20},{20... | collective-permute-start | bytes 1179656 | tf_op jit(solution)/shard_map/ppermute | solution.py:410
  63.7 24.3 %collective-permute-start.4 = (f32[2,96,256]{2,1,0:T(8,128)S(1)}, f32[2,96,256]{2,1,0:T(8,128)S(1)}, u32[]{:S(2)}, u32[]{:S(2)}) collective-permute-start(f32[2,96,256]{2,1,0:T(8,128)S(1)} %get-tuple-element.31), channel_id=1, source_target_pairs={{0,32},{32,0},{1,33},{33,1},{2,34},{34,2},{3,35},{35,3},{4,36},{36... | collective-permute-start | bytes 589832 | tf_op jit(solution)/shard_map/ppermute | solution.py:410
  81.5 15.6 %all-to-all-start.3 = ((f32[64,2,128]{2,1,0:T(2,128)}), f32[64,2,128]{2,1,0:T(2,128)S(1)}, u32[]{:S(2)}, u32[]{:S(2)}) async-start(f32[64,2,128]{2,1,0:T(2,128)} %square_sums.1), calls=%async_computation.3 | async-start | bytes 131072 | tf_op jit(solution)/shard_map/all_to_all | solution.py:430
